TPU v7x, 256 devices: a whole 4x4x8 slice. The times are simulated.
256 devices in a mesh: tm: 8 (over z), chan: 32 (over y, x, core).
Axes of the slice: x: 4, y: 4, z: 8, core: 2. Of those that a mesh axis runs over, the one named last changes fastest.
Arguments:
- raw: bfloat16 [12288, 16384], P(('tm', 'chan')), may hold values from -6 to 6
- band_taps: bfloat16 [128], replicated, may hold values from -0.5 to 0.5
- real_taps: bfloat16 [128], replicated, may hold values from -0.5 to 0.5
- imag_taps: bfloat16 [128], replicated, may hold values from -0.5 to 0.5
- short_taps: bfloat16 [128], replicated, may hold values from 0.0039978027 to 0.011962891
- lta_rate: float32 [16384], P('chan'), may hold values from 1.6276042e-06 to 0.03125
- lta_start: float32 [16384], P('chan'), may hold values from 0.5 to 4
- gap_gain: float32 [12288], P('tm'), may hold values from 0.5 to 1
Outputs:
- ratio: float32 [12288, 16384], P('tm', 'chan')
All inputs are finite; a program needn't handle non-finite values.
Results may differ from a plain program's by a relative error of at most 0.00091.
Values may be sent and summed in bfloat16 or wider, within the bound.
No kernel may reach another device: no remote copies, remote signals or barrier semaphores. Data moves between devices by JAX's collectives and lax.ppermute only.
A program may use at most 64 MiB of HBM per device.

v0:
```python
import jax
import jax.numpy as jnp
from jax import lax
from jax.sharding import PartitionSpec as P

BLOCK = 128


def from_behind(value, axis, steps):
    count = lax.axis_size(axis)
    leading, last = (max(0, -steps), min(count, count - steps))
    return lax.ppermute(value, axis, [(source, source + steps) for source in range(leading, last)])


def prefix(x, axis, combine, identity):
    count, position = (lax.axis_size(axis), lax.axis_index(axis))
    everything = jax.tree.map(lambda part: lax.all_gather(part, axis), x)
    start = jax.tree.map(
        lambda part, zero: jnp.broadcast_to(jnp.asarray(zero, part.dtype), part.shape), x, identity
    )

    def hop(k, before):
        reached = k < position
        new = combine(before, jax.tree.map(lambda part: part[k], everything))
        return jax.tree.map(lambda a, b: jnp.where(reached, a, b), new, before)

    return lax.fori_loop(0, count, hop, start)


def band_matrices(taps):
    lag = jnp.arange(BLOCK)[:, None] - jnp.arange(BLOCK)[None, :]
    picks = jnp.arange(BLOCK)
    weights = taps.astype(jnp.float32)
    current = jnp.sum(jnp.where(lag[:, :, None] == picks[None, None, :], weights, 0.0), axis=2)
    earlier = jnp.sum(
        jnp.where((lag + BLOCK)[:, :, None] == picks[None, None, :], weights, 0.0), axis=2
    )
    return (current.astype(taps.dtype), earlier.astype(taps.dtype))


def block_filter(signal, taps, history):
    current, earlier = band_matrices(taps)
    rows, cols = signal.shape
    blocks = signal.reshape(rows // BLOCK, BLOCK, cols)
    prior = jnp.concatenate([history[None], blocks[:-1]], axis=0)
    out = jnp.einsum("ij,bjc->bic", current, blocks, preferred_element_type=jnp.float32)
    out = out + jnp.einsum("ij,bjc->bic", earlier, prior, preferred_element_type=jnp.float32)
    return out.reshape(rows, cols)


def pair_energy(band, real_taps, imag_taps, history):
    real_part = block_filter(band, real_taps, history)
    imag_part = block_filter(band, imag_taps, history)
    return (real_part * real_part + imag_part * imag_part).astype(jnp.bfloat16)


def combine_pairs(earlier_pair, later_pair):
    return (earlier_pair[0] * later_pair[0], later_pair[0] * earlier_pair[1] + later_pair[1])


def body(raw, band_taps, real_taps, imag_taps, short_taps, lta_rate, lta_start, gap_gain):
    signal = lax.all_to_all(raw, "chan", split_axis=1, concat_axis=0, tiled=True)
    rows, cols = signal.shape
    raw_prior = from_behind(signal[rows - BLOCK :], "tm", 1)
    band = block_filter(signal, band_taps, raw_prior).astype(jnp.bfloat16)
    band_prior = from_behind(band[rows - BLOCK :], "tm", 1)
    energy = pair_energy(band, real_taps, imag_taps, band_prior)
    energy_prior = from_behind(energy[rows - BLOCK :], "tm", 1)
    short = block_filter(energy, short_taps, energy_prior)
    count = rows // BLOCK
    keep_log = jnp.log(1.0 - lta_rate)
    gain_log = jnp.cumsum(jnp.log(gap_gain).reshape(count, BLOCK), axis=1)
    offsets = jnp.arange(1, BLOCK + 1, dtype=jnp.float32)
    power = offsets[None, :, None] * keep_log[None, None, :] + gain_log[:, :, None]
    growth = jnp.exp(power)
    scaled = jnp.exp(-power) * lta_rate * energy.reshape(count, BLOCK, cols).astype(jnp.float32)
    lower = (jnp.arange(BLOCK)[:, None] >= jnp.arange(BLOCK)[None, :]).astype(jnp.float32)
    running = jnp.einsum("ij,bjc->bic", lower, scaled, precision=lax.Precision.HIGHEST)
    end_decay = growth[:, BLOCK - 1, :]
    end_value = end_decay * running[:, BLOCK - 1, :]
    ones = jnp.ones((cols,), jnp.float32)
    zeros = jnp.zeros((cols,), jnp.float32)

    def compose(state, block_pair):
        return (combine_pairs(state, block_pair), state)

    totals, prefixes = lax.scan(compose, (ones, zeros), (end_decay, end_value))
    before_decay, before_value = prefix(totals, "tm", combine_pairs, (ones, zeros))
    carry_in = before_decay * lta_start + before_value
    block_carry = prefixes[0] * carry_in[None, :] + prefixes[1]
    long_avg = (growth * (block_carry[:, None, :] + running)).reshape(rows, cols)
    return short / long_avg


def solution(mesh):
    return jax.shard_map(
        body,
        mesh=mesh,
        in_specs=(P(("tm", "chan"), None), P(), P(), P(), P(), P("chan"), P("chan"), P("tm")),
        out_specs=P("tm", "chan"),
        check_vma=False,
    )
```

profile of v0, /device:TPU:2, one launch (start us, length us, event | category | flops | bytes accessed | tf_op | source)
XLA Modules:
  0.0 122.8 jit_solution(12142822659946838880)
XLA Ops:
  0.0 2.8 %copy.97 = bf16[6,32,8,512]{3,2,0,1:T(8,128)(2,1)} copy(bf16[6,32,8,512]{3,2,1,0:T(8,128)(2,1)} %bitcast.91) | data formatting | bytes 3145728 | tf_op jit(solution)/shard_map/all_to_all | solution.py:62
  2.9 7.6 %all-to-all-start = ((bf16[48,32,512]{2,0,1:T(8,128)(2,1)}), bf16[48,32,512]{2,0,1:T(8,128)(2,1)S(1)}, u32[]{:S(2)}, u32[]{:S(2)}) async-start(bf16[48,32,512]{2,0,1:T(8,128)(2,1)} %bitcast.73), calls=%async_computation | async-start | bytes 3145728 | tf_op jit(solution)/shard_map/all_to_all | solution.py:62
  10.7 0.3 reduce_window_sum.14
  11.0 0.1 broadcast_multiply_fusion
  11.1 0.4 add_exponential_fusion
  11.5 1.7 %slice_reduce_fusion.1 = f32[12,512]{1,0:T(8,128)S(1)} fusion(f32[12,128,512]{1,2,0:T(8,128)S(1)} %add_exponential_fusion), kind=kLoop, calls=%fused_computation.26 | loop fusion | bytes 49152 | tf_op jit(solution)/shard_map/slice | solution.py:79
  13.3 23.5 %select_reduce_fusion.1 = (bf16[128,128]{1,0:T(8,128)(2,1)S(1)}, bf16[128,128]{1,0:T(8,128)(2,1)S(1)}, bf16[128,128]{1,0:T(8,128)(2,1)S(1)}, bf16[128,128]{1,0:T...) fusion(f32[128]{0:T(128)S(1)} %convert_element_type.66, ...), kind=kLoop, calls=%fused_computation.10 | loop fusion | flops 37617664 | bytes 395264 | tf_op jit(solution)/shard_map/reduce_sum | solution.py:34
  36.8 3.8 %collective-permute-start = (bf16[128,512]{1,0:T(8,128)(2,1)S(1)}, bf16[128,512]{1,0:T(8,128)(2,1)S(1)}, u32[]{:S(2)}, u32[]{:S(2)}) collective-permute-start(bf16[128,512]{1,0:T(8,128)(2,1)S(1)} %slice.45), channel_id=1, source_target_pairs={{0,32},{32,64},{64,96},{96,128},{128,160},{160,192},{192,224},{1,3... | collective-permute-start | bytes 393224 | tf_op jit(solution)/shard_map/ppermute | solution.py:12
  40.7 0.6 fusion.33
  41.2 0.2 slice.46
  41.4 2.3 %collective-permute-done = bf16[128,512]{1,0:T(8,128)(2,1)S(1)} collective-permute-done((bf16[128,512]{1,0:T(8,128)(2,1)S(1)}, bf16[128,512]{1,0:T(8,128)(2,1)S(1)}, u32[]{:S(2)}, u32[]{:S(2)}) %collective-permute-start) | collective-permute-done | bytes 131104 | tf_op jit(solution)/shard_map/ppermute | solution.py:12
  43.7 0.6 fusion.5
  44.3 0.6 fusion.27
  44.9 4.4 %collective-permute-start.1 = (bf16[128,512]{1,0:T(8,128)(2,1)S(1)}, bf16[128,512]{1,0:T(8,128)(2,1)S(1)}, u32[]{:S(2)}, u32[]{:S(2)}) collective-permute-start(bf16[128,512]{1,0:T(8,128)(2,1)S(1)} %slice_bitcast_fusion.1), channel_id=1, source_target_pairs={{0,32},{32,64},{64,96},{96,128},{128,160},{160,192},{192,224},{1,3... | collective-permute-start | bytes 393224 | tf_op jit(solution)/shard_map/ppermute | solution.py:12
  49.3 0.6 fusion.30
  49.9 0.2 slice.48
  50.1 1.7 %collective-permute-done.1 = bf16[128,512]{1,0:T(8,128)(2,1)S(1)} collective-permute-done((bf16[128,512]{1,0:T(8,128)(2,1)S(1)}, bf16[128,512]{1,0:T(8,128)(2,1)S(1)}, u32[]{:S(2)}, u32[]{:S(2)}) %collective-permute-start.1) | collective-permute-done | bytes 131104 | tf_op jit(solution)/shard_map/ppermute | solution.py:12
  51.8 0.6 fusion.20
  52.4 1.0 fusion.19
  53.5 2.2 %fusion.7 = f32[12,128,512]{1,2,0:T(8,128)S(1)} fusion(bf16[12,128,512]{1,2,0:T(8,128)(2,1)S(1)} %fusion.19, f32[512]{0:T(512)S(1)} %copy-done.2, f32[12,128]{1,0:T(8,128)S(1)} %reduce_window_sum.14, f32[128,512]{0,1:T(8,128)S(1)} %broadcast_multiply_fusion), kind=kOutput, calls=%fused_computation.32 | convolution fusion | flops 1211908096 | bytes 4988928 | tf_op jit(solution)/shard_map/ij,bjc->bic/dot_general | solution.py:78
  55.7 2.7 %fusion.24 = f32[12,512,128]{2,1,0:T(8,128)} fusion(bf16[12,128,512]{1,2,0:T(8,128)(2,1)S(1)} %fusion.19, bf16[128,128]{1,0:T(8,128)(2,1)S(1)} %get-tuple-element.210), kind=kOutput, calls=%fused_computation.53 | convolution fusion | flops 201326592 | bytes 4751360 | tf_op jit(solution)/shard_map/ij,bjc->bic/dot_general | solution.py:46
  58.4 4.7 %collective-permute-start.2 = (bf16[128,512]{0,1:T(8,128)(2,1)S(1)}, bf16[128,512]{0,1:T(8,128)(2,1)S(1)}, u32[]{:S(2)}, u32[]{:S(2)}) collective-permute-start(bf16[128,512]{0,1:T(8,128)(2,1)S(1)} %slice_bitcast_fusion), channel_id=1, source_target_pairs={{0,32},{32,64},{64,96},{96,128},{128,160},{160,192},{192,224},{1,3... | collective-permute-start | bytes 393224 | tf_op jit(solution)/shard_map/ppermute | solution.py:12
  63.1 1.7 %slice_reduce_fusion = f32[12,512]{1,0:T(8,128)S(1)} fusion(f32[12,128,512]{1,2,0:T(8,128)S(1)} %fusion.7), kind=kLoop, calls=%fused_computation.25 | loop fusion | bytes 49152 | tf_op jit(solution)/shard_map/slice | solution.py:80
  64.8 2.4 %while.33 = (s32[]{:T(128)}, f32[512]{0:T(512)S(1)}, f32[512]{0:T(512)S(1)}, f32[12,512]{1,0:T(8,128)S(1)}, f32[12,512]{1,0:T(8,128)S(1)}, /*index=5*/f32[12,512...) while((s32[]{:T(128)}, f32[512]{0:T(512)S(1)}, f32[512]{0:T(512)S(1)}, ...), condition=%wide.region_10.11_spmd.clone, body=%wide.region_9.10_spmd.clone.sunk | while | flops 2563 | bytes 32891 | solution.py:87
  64.8 0.1 dynamic_update_slice.11
  64.9 0.1 dynamic_update_slice.12
  65.0 0.1 dynamic_update_slice.11
  65.1 0.1 dynamic_update_slice.12
  65.2 0.1 dynamic_update_slice.11
  65.3 0.1 dynamic_update_slice.12
  65.4 0.1 dynamic_update_slice.11
  65.5 0.1 dynamic_update_slice.12
  65.6 0.1 dynamic_update_slice.11
  65.7 0.1 dynamic_update_slice.12
  65.8 0.1 dynamic_update_slice.11
  65.9 0.1 dynamic_update_slice.12
  66.0 0.1 dynamic_update_slice.11
  66.1 0.1 dynamic_update_slice.12
  66.4 0.1 dynamic_update_slice.11
  66.6 0.1 dynamic_update_slice.11
  66.7 0.1 dynamic_update_slice.12
  66.9 0.1 dynamic_update_slice.12
  67.0 0.1 dynamic_update_slice.11
  67.2 25.9 %all-gather.2 = f32[8,1,512]{2,1,0:T(1,128)S(1)} all-gather(f32[1,1,512]{2,1,0:T(1,128)S(1)} %bitcast.101), channel_id=2, replica_groups=mesh['tm'=8,'chan'=32] {'tm'}, dimensions={0}, use_global_device_ids=true | all-gather | bytes 18432 | tf_op jit(solution)/shard_map/all_gather | solution.py:17
  93.1 21.1 %all-gather.3 = f32[8,1,512]{2,1,0:T(1,128)S(1)} all-gather(f32[1,1,512]{2,1,0:T(1,128)S(1)} %bitcast.102), channel_id=3, replica_groups=mesh['tm'=8,'chan'=32] {'tm'}, dimensions={0}, use_global_device_ids=true | all-gather | bytes 18432 | tf_op jit(solution)/shard_map/all_gather | solution.py:17
  114.2 0.5 while.34
  114.7 4.6 %bitcast_divide_fusion = f32[12,128,512]{1,2,0:T(8,128)} fusion(f32[12,128,512]{1,2,0:T(8,128)} %copy-done.1, f32[12,512,128]{2,1,0:T(8,128)} %fusion.24, bf16[11,128,512]{1,2,0:T(8,128)(2,1)S(1)} %slice-done, bf16[1,128,512]{1,2,0:T(8,128)(2,1)S(1)} %bitcast.105, f32[12,512]{1,0:T(8,128)S(1)} %multiply_add_fusion.1, f32[12,128]{1,0:T(8,128)S(1)} %reduce_window_sum.14, ...), kind=kOutput, calls=%fused_computation.27 | convolution fusion | flops 206045184 | bytes 11335680 | tf_op jit(solution)/shard_map/ij,bjc->bic/dot_general | solution.py:47
  119.3 3.5 %copy.78 = f32[12,128,512]{2,1,0:T(8,128)} copy(f32[12,128,512]{1,2,0:T(8,128)} %bitcast_divide_fusion) | data formatting | bytes 6291456 | tf_op jit(solution)/shard_map/div | solution.py:92
  (89 shorter events, 1.0 us)
Async XLA Ops:
  0.0 10.6 %copy-start.5 = (bf16[128]{0:T(256)(128)(2,1)S(1)}, bf16[128]{0:T(256)(128)(2,1)}, u32[]{:S(2)}) copy-start(bf16[128]{0:T(256)(128)(2,1)} %param.16) | copy-start | bytes 772
  0.0 10.6 %copy-start.6 = (bf16[128]{0:T(256)(128)(2,1)S(1)}, bf16[128]{0:T(256)(128)(2,1)}, u32[]{:S(2)}) copy-start(bf16[128]{0:T(256)(128)(2,1)} %param.15) | copy-start | bytes 772
  0.0 10.6 %copy-start.7 = (bf16[128]{0:T(256)(128)(2,1)S(1)}, bf16[128]{0:T(256)(128)(2,1)}, u32[]{:S(2)}) copy-start(bf16[128]{0:T(256)(128)(2,1)} %param.14) | copy-start | bytes 772
  0.0 10.6 %copy-start.8 = (bf16[128]{0:T(256)(128)(2,1)S(1)}, bf16[128]{0:T(256)(128)(2,1)}, u32[]{:S(2)}) copy-start(bf16[128]{0:T(256)(128)(2,1)} %param.13) | copy-start | bytes 772
  0.0 10.6 %copy-start.3 = (f32[1536]{0:T(1024)S(1)}, f32[1536]{0:T(1024)}, u32[]{:S(2)}) copy-start(f32[1536]{0:T(1024)} %param.19) | copy-start | bytes 18436
  0.0 10.6 %copy-start.2 = (f32[512]{0:T(512)S(1)}, f32[512]{0:T(512)}, u32[]{:S(2)}) copy-start(f32[512]{0:T(512)} %param.17) | copy-start | bytes 6148
  2.9 33.9 %all-to-all-start = ((bf16[48,32,512]{2,0,1:T(8,128)(2,1)}), bf16[48,32,512]{2,0,1:T(8,128)(2,1)S(1)}, u32[]{:S(2)}, u32[]{:S(2)}) async-start(bf16[48,32,512]{2,0,1:T(8,128)(2,1)} %bitcast.73), calls=%async_computation | async-start | bytes 3145728 | tf_op jit(solution)/shard_map/all_to_all | solution.py:62
  36.8 6.9 %collective-permute-start = (bf16[128,512]{1,0:T(8,128)(2,1)S(1)}, bf16[128,512]{1,0:T(8,128)(2,1)S(1)}, u32[]{:S(2)}, u32[]{:S(2)}) collective-permute-start(bf16[128,512]{1,0:T(8,128)(2,1)S(1)} %slice.45), channel_id=1, source_target_pairs={{0,32},{32,64},{64,96},{96,128},{128,160},{160,192},{192,224},{1,3... | collective-permute-start | bytes 393224 | tf_op jit(solution)/shard_map/ppermute | solution.py:12
  44.9 6.9 %collective-permute-start.1 = (bf16[128,512]{1,0:T(8,128)(2,1)S(1)}, bf16[128,512]{1,0:T(8,128)(2,1)S(1)}, u32[]{:S(2)}, u32[]{:S(2)}) collective-permute-start(bf16[128,512]{1,0:T(8,128)(2,1)S(1)} %slice_bitcast_fusion.1), channel_id=1, source_target_pairs={{0,32},{32,64},{64,96},{96,128},{128,160},{160,192},{192,224},{1,3... | collective-permute-start | bytes 393224 | tf_op jit(solution)/shard_map/ppermute | solution.py:12
  53.4 2.3 %copy-start = (bf16[12,128,512]{1,2,0:T(8,128)(2,1)}, bf16[12,128,512]{1,2,0:T(8,128)(2,1)S(1)}, u32[]{:S(2)}) copy-start(bf16[12,128,512]{1,2,0:T(8,128)(2,1)S(1)} %fusion.19) | copy-start | bytes 4718596
  55.7 7.4 %copy-start.1 = (f32[12,128,512]{1,2,0:T(8,128)}, f32[12,128,512]{1,2,0:T(8,128)S(1)}, u32[]{:S(2)}) copy-start(f32[12,128,512]{1,2,0:T(8,128)S(1)} %fusion.7) | copy-start | bytes 9437188
  58.4 56.3 %copy-start.4 = (f32[512]{0:T(512)S(1)}, f32[512]{0:T(512)}, u32[]{:S(2)}) copy-start(f32[512]{0:T(512)} %param.18) | copy-start | bytes 6148
  58.4 56.3 %slice-start = ((bf16[12,128,512]{1,2,0:T(8,128)(2,1)}), bf16[11,128,512]{1,2,0:T(8,128)(2,1)S(1)}, s32[]{:S(2)}) async-start(bf16[12,128,512]{1,2,0:T(8,128)(2,1)} %copy-done), calls=%async_computation.1 | async-start | bytes 2883584 | tf_op jit(solution)/shard_map/slice | solution.py:45
  58.4 56.3 %collective-permute-start.2 = (bf16[128,512]{0,1:T(8,128)(2,1)S(1)}, bf16[128,512]{0,1:T(8,128)(2,1)S(1)}, u32[]{:S(2)}, u32[]{:S(2)}) collective-permute-start(bf16[128,512]{0,1:T(8,128)(2,1)S(1)} %slice_bitcast_fusion), channel_id=1, source_target_pairs={{0,32},{32,64},{64,96},{96,128},{128,160},{160,192},{192,224},{1,3... | collective-permute-start | bytes 393224 | tf_op jit(solution)/shard_map/ppermute | solution.py:12
where the time goes:
time: 123 us
  blocking collectives  47 us (38%)
  other arithmetic  24.7 us (20%)
  starting transfers between devices  20.5 us (17%)
  matrix products  13.4 us (11%)
  local copies, waits for them, and re-layouts  11.9 us (10%)
  waiting for transfers between devices  4.06 us (3%)
    all_gather x2, blocking collectives, prefix(): everything = jax.tree.map(lambda part: lax.all_gather(part, axis), x)  47 us
    reduce_sum x1, other arithmetic, band_matrices(): jnp.sum(jnp.where(lag[:, :, None] == picks[None, None, :], weights, 0.0),...  23.5 us
    ppermute x3, starting transfers between devices, from_behind(): lax.ppermute(value, axis, [(source, source + steps) for source in range(l...  12.9 us
    all_to_all x1, starting transfers between devices, body(): lax.all_to_all(raw, 'chan', split_axis=1, concat_axis=0, tiled=True)  7.62 us
    dot_general x4, matrix products, block_filter(): jnp.einsum('ij,bjc->bic', earlier, prior, preferred_element_type=jnp.floa...  6.79 us
    dot_general x4, matrix products, block_filter(): jnp.einsum('ij,bjc->bic', current, blocks, preferred_element_type=jnp.flo...  4.43 us
    ppermute x3, waiting for transfers between devices, from_behind(): lax.ppermute(value, axis, [(source, source + steps) for source in range(l...  4.05 us
    div x1, local copies, waits for them, and re-layouts, body(): return short / long_avg  3.54 us
  transfers between devices with their start and end apart: 4, of which 2 were waited for; matrix products, arithmetic and copies ran while one was open for 26% of the time, Pallas kernels for 0%

commit v1 on v0

v1 whole, which is shorter than its diff:
```python
import functools

import jax
import jax.numpy as jnp
from jax import lax
from jax.experimental import pallas as pl
from jax.experimental.pallas import tpu as pltpu
from jax.sharding import PartitionSpec as P

BLOCK = 128
SUB = 64
VMEM = pl.BlockSpec(memory_space=pltpu.VMEM)
SMEM = pl.BlockSpec(memory_space=pltpu.SMEM)


def dot(a, b):
    return jnp.dot(a, b, preferred_element_type=jnp.float32)


def call(kernel, out_shape, in_specs, out_specs=None, scratch=(), limit=24):
    if out_specs is None:
        out_specs = jax.tree.map(lambda _: VMEM, out_shape)
    return pl.pallas_call(
        kernel,
        out_shape=out_shape,
        in_specs=in_specs,
        out_specs=out_specs,
        scratch_shapes=scratch,
        compiler_params=pltpu.CompilerParams(vmem_limit_bytes=limit * 1024 * 1024),
    )


def from_behind(value, axis):
    count = lax.axis_size(axis)
    return lax.ppermute(value, axis, [(source, source + 1) for source in range(count - 1)])


def matrices_kernel(rows_ref, band_ref, pair_ref, short_ref, sums_ref):
    def toeplitz(k):
        row = jnp.broadcast_to(rows_ref[k : k + 1, :], (BLOCK, 2 * BLOCK))
        return pltpu.roll(row, 0, 1, stride=1, stride_axis=0).astype(jnp.bfloat16)

    band_ref[...] = toeplitz(0)
    pair_ref[:BLOCK, :] = toeplitz(1)
    pair_ref[BLOCK:, :] = toeplitz(2)
    short_ref[...] = toeplitz(3)
    row = lax.broadcasted_iota(jnp.int32, (BLOCK, 2 * BLOCK), 0)
    col = lax.broadcasted_iota(jnp.int32, (BLOCK, 2 * BLOCK), 1) % BLOCK
    keep = (col <= row) & (col // SUB == row // SUB)
    sums_ref[...] = jnp.where(keep, 1.0, 0.0).astype(jnp.bfloat16)


def energy_of(pair, window):
    both = dot(pair, window)
    real, imag = both[:BLOCK], both[BLOCK:]
    return (real * real + imag * imag).astype(jnp.bfloat16)


def lanes(column, cols):
    return jnp.concatenate([column] * (cols // 128), axis=1)


def running_of(energy, sums, rate_scale, gain_scale):
    cols = energy.shape[1]
    scaled = energy.astype(jnp.float32) * rate_scale * lanes(gain_scale, cols)
    high = scaled.astype(jnp.bfloat16)
    low = (scaled - high.astype(jnp.float32)).astype(jnp.bfloat16)
    return dot(sums, jnp.concatenate([high, low], axis=0))


def short_of(short, window, scale, gain_scale):
    return dot(short, window) * scale * lanes(gain_scale, window.shape[1])


def main_kernel(
    count, signal, band_m, pair_m, short_m, sums_m, rate_scale, scale, gain_scale,
    band1, energy2, energy_last, running, upper, band, energy,
):
    def rows(b, n=1):
        return pl.ds(pl.multiple_of(b * BLOCK, BLOCK), n * BLOCK)

    def band_step(b, _):
        band[rows(b), :] = dot(band_m[...], signal[rows(b - 1, 2), :]).astype(jnp.bfloat16)
        return 0

    lax.fori_loop(1, count, band_step, 0, unroll=True)

    def energy_step(b, _):
        e = energy_of(pair_m[...], band[rows(b - 1, 2), :])
        energy[rows(b), :] = e
        running[rows(b - 2), :] = running_of(e, sums_m[...], rate_scale[...], gain_scale[rows(b), :])
        return 0

    lax.fori_loop(2, count, energy_step, 0, unroll=True)

    def short_step(b, _):
        upper[rows(b - 3), :] = short_of(
            short_m[...], energy[rows(b - 1, 2), :], scale[...], gain_scale[rows(b), :]
        )
        return 0

    lax.fori_loop(3, count, short_step, 0, unroll=True)
    band1[...] = band[rows(1), :]
    energy2[...] = energy[rows(2), :]
    energy_last[...] = energy[rows(count - 1), :]


def edge_kernel(
    subs, prior, signal, band1, energy2, running, band_m, pair_m, short_m, sums_m,
    rate_scale, scale, gain_scale, ends,
    energy0, running01, upper12, totals,
):
    h1 = prior[BLOCK:, :]
    band_before = dot(band_m[...], prior[...]).astype(jnp.bfloat16)
    band0 = dot(band_m[...], jnp.concatenate([h1, signal[:BLOCK, :]], axis=0)).astype(jnp.bfloat16)
    e0 = energy_of(pair_m[...], jnp.concatenate([band_before, band0], axis=0))
    e1 = energy_of(pair_m[...], jnp.concatenate([band0, band1[...]], axis=0))
    energy0[...] = e0
    run0 = running_of(e0, sums_m[...], rate_scale[...], gain_scale[:BLOCK, :])
    run1 = running_of(e1, sums_m[...], rate_scale[...], gain_scale[BLOCK : 2 * BLOCK, :])
    running01[:BLOCK, :] = run0
    running01[BLOCK:, :] = run1
    upper12[:BLOCK, :] = short_of(
        short_m[...], jnp.concatenate([e0, e1], axis=0), scale[...], gain_scale[BLOCK : 2 * BLOCK, :]
    )
    upper12[BLOCK:, :] = short_of(
        short_m[...],
        jnp.concatenate([e1, energy2[...]], axis=0),
        scale[...],
        gain_scale[2 * BLOCK : 3 * BLOCK, :],
    )
    first = (run0, run1)
    value = jnp.zeros_like(ends[0:1, :])
    decay = jnp.ones_like(value)
    for s in range(subs):
        last = (s % 2) * SUB + SUB - 1
        if s < 4:
            end = first[s // 2][last : last + 1, :]
        else:
            end = running[s * SUB - 2 * BLOCK + SUB - 1 : s * SUB - 2 * BLOCK + SUB, :]
        step = ends[s : s + 1, :]
        value = step * (value + end)
        decay = decay * step
    both = jnp.concatenate([decay, value], axis=0)
    for k in range(totals.shape[0]):
        totals[k] = both


def ratio_kernel(
    subs, chunks, position, totals, start, energy_before, energy0, running01, running, upper12, upper,
    short_m, scale, gain_scale, ends, out, buffer, sems,
):
    state = start[...]
    for k in range(totals.shape[0]):
        new = totals[k, 0:1, :] * state + totals[k, 1:2, :]
        state = jnp.where(k < position[0], new, state)
    upper0 = short_of(
        short_m[...],
        jnp.concatenate([energy_before[...], energy0[...]], axis=0),
        scale[...],
        gain_scale[:BLOCK, :],
    )
    rows = subs * SUB // chunks
    copies = []
    for s in range(subs):
        at = s * SUB
        if at < 2 * BLOCK:
            run = running01[at : at + SUB, :]
        else:
            run = running[at - 2 * BLOCK : at - 2 * BLOCK + SUB, :]
        if at < BLOCK:
            top = upper0[at : at + SUB, :]
        elif at < 3 * BLOCK:
            top = upper12[at - BLOCK : at - BLOCK + SUB, :]
        else:
            top = upper[at - 3 * BLOCK : at - 3 * BLOCK + SUB, :]
        buffer[at : at + SUB, :] = top / (run + state)
        state = ends[s : s + 1, :] * (state + run[SUB - 1 : SUB, :])
        if (at + SUB) % rows == 0:
            c = at // rows
            part = pl.ds(c * rows, rows)
            copy = pltpu.make_async_copy(buffer.at[part, :], out.at[part, :], sems.at[c])
            copy.start()
            copies.append(copy)
    for copy in copies:
        copy.wait()


def body(raw, band_taps, real_taps, imag_taps, short_taps, lta_rate, lta_start, gap_gain):
    f32, bf16 = jnp.float32, jnp.bfloat16
    struct = jax.ShapeDtypeStruct
    signal = lax.all_to_all(raw, "chan", split_axis=1, concat_axis=0, tiled=True)
    total, cols = signal.shape
    count, subs = total // BLOCK, total // SUB
    groups = lax.axis_size("tm")

    taps = jnp.stack([band_taps, real_taps, imag_taps, short_taps]).astype(f32)
    tap_rows = jnp.pad(taps[:, ::-1], ((0, 0), (1, BLOCK - 1)))
    band_m, pair_m, short_m, sums_m = call(
        matrices_kernel,
        [
            struct((BLOCK, 2 * BLOCK), bf16),
            struct((2 * BLOCK, 2 * BLOCK), bf16),
            struct((BLOCK, 2 * BLOCK), bf16),
            struct((BLOCK, 2 * BLOCK), bf16),
        ],
        [VMEM],
    )(tap_rows)

    keep_log = jnp.log1p(-(1.0 - (1.0 - lta_rate)))
    offsets = (jnp.arange(BLOCK) % SUB + 1).astype(f32)
    scale = jnp.exp(-offsets[:, None] * keep_log[None, :])
    rate_scale = scale * lta_rate[None, :]
    gain = jnp.cumprod(gap_gain.reshape(subs, SUB), axis=1)
    gain_scale = jnp.broadcast_to((1.0 / gain).reshape(total, 1), (total, 128))
    ends = jnp.exp(SUB * keep_log)[None, :] * gain[:, SUB - 1 :]

    prior = from_behind(signal[total - 2 * BLOCK :], "tm")
    band1, energy2, energy_last, running, upper = call(
        functools.partial(main_kernel, count),
        [
            struct((BLOCK, cols), bf16),
            struct((BLOCK, cols), bf16),
            struct((BLOCK, cols), bf16),
            struct((total - 2 * BLOCK, cols), f32),
            struct((total - 3 * BLOCK, cols), f32),
        ],
        [VMEM] * 8,
        scratch=[pltpu.VMEM((total, cols), bf16), pltpu.VMEM((total, cols), bf16)],
    )(signal, band_m, pair_m, short_m, sums_m, rate_scale, scale, gain_scale)
    energy_before = from_behind(energy_last, "tm")
    energy0, running01, upper12, totals = call(
        functools.partial(edge_kernel, subs),
        [
            struct((BLOCK, cols), bf16),
            struct((2 * BLOCK, cols), f32),
            struct((2 * BLOCK, cols), f32),
            struct((groups, 2, cols), f32),
        ],
        [VMEM] * 13,
    )(prior, signal, band1, energy2, running, band_m, pair_m, short_m, sums_m,
      rate_scale, scale, gain_scale, ends)
    totals = lax.all_to_all(totals, "tm", split_axis=0, concat_axis=0, tiled=True)
    position = lax.axis_index("tm").astype(jnp.int32).reshape(1)
    chunks = 4
    return call(
        functools.partial(ratio_kernel, subs, chunks),
        struct((total, cols), f32),
        [SMEM] + [VMEM] * 12,
        out_specs=pl.BlockSpec(memory_space=pl.ANY),
        scratch=[pltpu.VMEM((total, cols), f32), pltpu.SemaphoreType.DMA((chunks,))],
    )(position, totals, lta_start.reshape(1, cols), energy_before, energy0, running01, running,
      upper12, upper, short_m, scale, gain_scale, ends)


def solution(mesh):
    return jax.shard_map(
        body,
        mesh=mesh,
        in_specs=(P(("tm", "chan"), None), P(), P(), P(), P(), P("chan"), P("chan"), P("tm")),
        out_specs=P("tm", "chan"),
        check_vma=False,
    )
```

time: 123 us -> 73.7 us (0.60)
  blocking collectives: 47 us -> 0 us
  waiting for transfers between devices: 4.06 us -> 29.4 us
  other arithmetic: 24.7 us -> 0.44 us
  matrix products: 13.4 us -> 0 us
  Pallas kernels: 0 us -> 8.74 us
  starting transfers between devices: 20.5 us -> 22.3 us
    all_gather x2 -> x0, blocking collectives: 47 us -> none  [prefix(): everything = jax.tree.map(lambda part: lax.all_gather(part, axis), x)]
    reduce_sum x1 -> x0, other arithmetic: 23.5 us -> none  [band_matrices(): jnp.sum(jnp.where(lag[:, :, None] == picks[None, None, :], weights, 0.0),...]
    all_to_all x1, waiting for transfers between devices: 0.01 us -> 21.4 us  [body(): lax.all_to_all(raw, 'chan', split_axis=1, concat_axis=0, tiled=True)]
    dot_general x9 -> x0, matrix products: 13.4 us -> none  [the longest x4 6.79 us: block_filter(): jnp.einsum('ij,bjc->bic', earlier, prior, preferred_element_type=jnp.floa...]
    pallas_call x0 -> x4, Pallas kernels: none -> 8.74 us  [the longest x1 4.24 us: body(): call(functools.partial(main_kernel, count), [struct((BLOCK, cols), bf16),...]
    unnamed x20 -> x34, local copies, waits for them, and re-layouts: 0.04 us -> 8.49 us
    all_to_all x0 -> x1, waiting for transfers between devices: none -> 8.02 us  [body(): lax.all_to_all(totals, 'tm', split_axis=0, concat_axis=0, tiled=True)]
    all_to_all x0 -> x1, starting transfers between devices: none -> 6.21 us  [body(): lax.all_to_all(totals, 'tm', split_axis=0, concat_axis=0, tiled=True)]
  transfers between devices with their start and end apart: 4 -> 4, of which waited for: 2 -> 2; matrix products, arithmetic and copies ran while one was open for 26% -> 2% of each run, Pallas kernels for 0% -> 8%
where the time goes in v1:
time: 73.7 us; the launch traced here: 73 us
  waiting for transfers between devices  29.4 us (40%)
  starting transfers between devices  22.3 us (30%)
  local copies, waits for them, and re-layouts  12 us (16%)
  Pallas kernels  8.74 us (12%)
    all_to_all x1, waiting for transfers between devices, body(): lax.all_to_all(raw, 'chan', split_axis=1, concat_axis=0, tiled=True)  21.4 us
    unnamed x34, local copies, waits for them, and re-layouts  8.49 us
    ppermute x2, starting transfers between devices, from_behind(): lax.ppermute(value, axis, [(source, source + 1) for source in range(count...  8.29 us
    all_to_all x1, waiting for transfers between devices, body(): lax.all_to_all(totals, 'tm', split_axis=0, concat_axis=0, tiled=True)  8.02 us
    all_to_all x1, starting transfers between devices, body(): lax.all_to_all(raw, 'chan', split_axis=1, concat_axis=0, tiled=True)  7.76 us
    all_to_all x1, starting transfers between devices, body(): lax.all_to_all(totals, 'tm', split_axis=0, concat_axis=0, tiled=True)  6.21 us
    pallas_call x1, Pallas kernels, body(): call(functools.partial(main_kernel, count), [struct((BLOCK, cols), bf16),...  4.24 us
    pallas_call x1, Pallas kernels, body(): call(functools.partial(ratio_kernel, subs, chunks), struct((total, cols),...  2.93 us
  transfers between devices with their start and end apart: 4, of which 2 were waited for; matrix products, arithmetic and copies ran while one was open for 2% of the time, Pallas kernels for 8%

profile of v1, /device:TPU:2, one launch (start us, length us, event | category | flops | bytes accessed | tf_op | source)
XLA Modules:
  0.0 73.0 jit_solution(2766185549003023197)
XLA Ops:
  0.0 2.8 %copy.13 = bf16[6,32,8,512]{3,2,0,1:T(8,128)(2,1)} copy(bf16[6,32,8,512]{3,2,1,0:T(8,128)(2,1)} %bitcast.17) | data formatting | bytes 3145728 | tf_op jit(solution)/shard_map/all_to_all | solution.py:192
  2.8 0.0 copy-start.12
  2.8 0.0 copy-start.11
  2.8 0.0 copy-start.13
  2.8 0.0 copy-start.14
  2.8 0.0 copy-start.15
  2.8 0.0 copy-start.16
  2.8 7.8 %all-to-all-start = ((bf16[48,32,512]{2,0,1:T(8,128)(2,1)}), bf16[48,32,512]{2,0,1:T(8,128)(2,1)S(1)}, u32[]{:S(2)}, u32[]{:S(2)}) async-start(bf16[48,32,512]{2,0,1:T(8,128)(2,1)} %bitcast.12), calls=%async_computation | async-start | bytes 3145728 | tf_op jit(solution)/shard_map/all_to_all | solution.py:192
  10.6 0.0 copy-done.12
  10.6 0.1 reshape.37
  10.6 0.2 reduce_window.9
  10.9 0.2 slice_reduce_fusion
  11.1 0.0 copy-done.11
  11.1 0.1 multiply_exponential_fusion
  11.2 21.4 %all-to-all-done = bf16[48,32,512]{2,0,1:T(8,128)(2,1)S(1)} async-done(((bf16[48,32,512]{2,0,1:T(8,128)(2,1)}), bf16[48,32,512]{2,0,1:T(8,128)(2,1)S(1)}, u32[]{:S(2)}, u32[]{:S(2)}) %all-to-all-start) | async-done | bytes 1572896 | tf_op jit(solution)/shard_map/all_to_all | solution.py:192
  32.6 3.8 %collective-permute-start = (bf16[256,512]{1,0:T(8,128)(2,1)S(1)}, bf16[256,512]{1,0:T(8,128)(2,1)S(1)}, u32[]{:S(2)}, u32[]{:S(2)}) collective-permute-start(bf16[256,512]{1,0:T(8,128)(2,1)S(1)} %slice.8), channel_id=1, source_target_pairs={{0,32},{32,64},{64,96},{96,128},{128,160},{160,192},{192,224},{1,3... | collective-permute-start | bytes 786440 | tf_op jit(solution)/shard_map/ppermute | solution.py:35
  36.5 0.0 copy-done.13
  36.5 0.0 copy-done.14
  36.5 0.0 copy-done.15
  36.5 0.0 copy-done.16
  36.5 0.1 rev.3
  36.6 0.1 div.15
  36.7 0.1 pad.4.rows_ref
  36.8 0.1 shard_map.82
  36.9 0.3 broadcast_in_dim.2.gain_scale
  37.2 4.2 %shard_map.83 = (bf16[128,512]{1,0:T(8,128)(2,1)S(1)}, bf16[128,512]{1,0:T(8,128)(2,1)S(1)}, bf16[128,512]{1,0:T(8,128)(2,1)}, f32[1280,512]{1,0:T(8,128)S(1)}, f32[1152,512]{1,0:T(8,128)S(1)}) custom-call(bf16[1536,512]{1,0:T(8,128)(2,1)S(1)} %bitcast.14, bf16[128,256]{1,0:T(8,128)(2,1)S(1)} %get-tuple-element.18.band_m, ...), custom_call_target="tpu_custom_call" | custom-call | tf_op jit(solution)/shard_map/pallas_call | solution.py:219
  41.4 0.0 copy-start
  41.4 0.0 copy-start.2
  41.4 4.5 %collective-permute-start.1 = (bf16[128,512]{1,0:T(8,128)(2,1)}, bf16[128,512]{1,0:T(8,128)(2,1)}, u32[]{:S(2)}, u32[]{:S(2)}) collective-permute-start(bf16[128,512]{1,0:T(8,128)(2,1)} %get-tuple-element.26), channel_id=1, source_target_pairs={{0,32},{32,64},{64,96},{96,128},{128,160},{160,192},{192,224},{1,3... | collective-permute-start | bytes 393224 | tf_op jit(solution)/shard_map/ppermute | solution.py:35
  45.9 0.1 broadcast_multiply_fusion.1.ends
  46.0 0.0 collective-permute-done.prior
  46.0 0.7 copy-done.6
  46.7 0.0 copy-start.7
  46.7 0.9 %copy-done.7 = bf16[256,512]{1,0:T(8,128)(2,1)S(1)} copy-done((bf16[256,512]{1,0:T(8,128)(2,1)S(1)}, bf16[256,512]{1,0:T(8,128)(2,1)}, u32[]{:S(2)}) %copy-start.7) | copy-done | bytes 262168
  47.6 1.4 %shard_map.84 = (bf16[128,512]{1,0:T(8,128)(2,1)S(1)}, f32[256,512]{1,0:T(8,128)S(1)}, f32[256,512]{1,0:T(8,128)S(1)}, f32[8,2,512]{2,1,0:T(2,128)}) custom-call(bf16[256,512]{1,0:T(8,128)(2,1)S(1)} %copy-done.7, bf16[1536,512]{1,0:T(8,128)(2,1)S(1)} %bitcast.15, bf16[128,512]{1,0:T(8,128)(2,1)S(1)} %get-tuple-element.22.band1, ...), custom_call_target="tpu_custom_call" | custom-call | tf_op jit(solution)/shard_map/pallas_call | solution.py:232
  49.0 0.0 copy-done
  49.1 0.0 copy-done.2
  49.1 0.8 %copy-done.4 = f32[256,512]{1,0:T(8,128)} copy-done((f32[256,512]{1,0:T(8,128)}, f32[256,512]{1,0:T(8,128)S(1)}, u32[]{:S(2)}) %copy-start.4) | copy-done | bytes 524312
  49.9 0.6 copy-done.8
  50.5 6.2 %all-to-all-start.1 = ((f32[8,2,512]{2,1,0:T(2,128)}), f32[8,2,512]{2,1,0:T(2,128)S(1)}, u32[]{:S(2)}, u32[]{:S(2)}) async-start(f32[8,2,512]{2,1,0:T(2,128)} %get-tuple-element.25), calls=%async_computation.1 | async-start | bytes 65536 | tf_op jit(solution)/shard_map/all_to_all | solution.py:243
  56.7 0.0 collective-permute-done.1.energy_before
  56.7 8.0 %all-to-all-done.1.totals = f32[8,2,512]{2,1,0:T(2,128)S(1)} async-done(((f32[8,2,512]{2,1,0:T(2,128)}), f32[8,2,512]{2,1,0:T(2,128)S(1)}, u32[]{:S(2)}, u32[]{:S(2)}) %all-to-all-start.1) | async-done | bytes 32800 | tf_op jit(solution)/shard_map/all_to_all | solution.py:243
  64.7 0.0 copy-done.10
  64.8 1.7 %copy-done.1 = f32[1280,512]{1,0:T(8,128)S(1)} copy-done((f32[1280,512]{1,0:T(8,128)S(1)}, f32[1280,512]{1,0:T(8,128)}, u32[]{:S(2)}) %copy-start.1) | copy-done | bytes 2621464
  66.5 1.7 %copy-done.3 = f32[1152,512]{1,0:T(8,128)S(1)} copy-done((f32[1152,512]{1,0:T(8,128)S(1)}, f32[1152,512]{1,0:T(8,128)}, u32[]{:S(2)}) %copy-start.3) | copy-done | bytes 2359320
  68.2 1.0 %copy-done.5 = f32[256,512]{1,0:T(8,128)S(1)} copy-done((f32[256,512]{1,0:T(8,128)S(1)}, f32[256,512]{1,0:T(8,128)}, u32[]{:S(2)}) %copy-start.5) | copy-done | bytes 524312
  69.2 0.9 %copy-done.9 = bf16[128,512]{1,0:T(8,128)(2,1)S(1)} copy-done((bf16[128,512]{1,0:T(8,128)(2,1)S(1)}, bf16[128,512]{1,0:T(8,128)(2,1)}, u32[]{:S(2)}) %copy-start.9) | copy-done | bytes 131096
  70.1 2.9 %shard_map.85 = f32[1536,512]{1,0:T(8,128)} custom-call(s32[1]{0:T(128)} %bitcast.position, f32[8,2,512]{2,1,0:T(2,128)S(1)} %all-to-all-done.1.totals, f32[1,512]{1,0:T(1,128)S(1)} %bitcast.16, bf16[128,512]{1,0:T(8,128)(2,1)} %collective-permute-done.1.energy_before, bf16[128,512]{1,0:T(8,128)(2,1)S(1)} %copy-done.9, ...), custom_call_target="tpu_custom_call" | custom-call | tf_op jit(solution)/shard_map/pallas_call | solution.py:246
  (13 shorter events, 0.1 us)
Async XLA Ops:
  2.8 7.8 %copy-start.12 = (f32[1536]{0:T(1024)S(1)}, f32[1536]{0:T(1024)}, u32[]{:S(2)}) copy-start(f32[1536]{0:T(1024)} %param.15) | copy-start | bytes 18436
  2.8 8.3 %copy-start.11 = (f32[512]{0:T(512)S(1)}, f32[512]{0:T(512)}, u32[]{:S(2)}) copy-start(f32[512]{0:T(512)} %param.13) | copy-start | bytes 6148
  2.8 33.7 %copy-start.13 = (bf16[128]{0:T(256)(128)(2,1)S(1)}, bf16[128]{0:T(256)(128)(2,1)}, u32[]{:S(2)}) copy-start(bf16[128]{0:T(256)(128)(2,1)} %param.12) | copy-start | bytes 772
  2.8 33.7 %copy-start.14 = (bf16[128]{0:T(256)(128)(2,1)S(1)}, bf16[128]{0:T(256)(128)(2,1)}, u32[]{:S(2)}) copy-start(bf16[128]{0:T(256)(128)(2,1)} %param.11) | copy-start | bytes 772
  2.8 33.7 %copy-start.15 = (bf16[128]{0:T(256)(128)(2,1)S(1)}, bf16[128]{0:T(256)(128)(2,1)}, u32[]{:S(2)}) copy-start(bf16[128]{0:T(256)(128)(2,1)} %param.10) | copy-start | bytes 772
  2.8 33.7 %copy-start.16 = (bf16[128]{0:T(256)(128)(2,1)S(1)}, bf16[128]{0:T(256)(128)(2,1)}, u32[]{:S(2)}) copy-start(bf16[128]{0:T(256)(128)(2,1)} %param.9) | copy-start | bytes 772
  2.8 29.8 %all-to-all-start = ((bf16[48,32,512]{2,0,1:T(8,128)(2,1)}), bf16[48,32,512]{2,0,1:T(8,128)(2,1)S(1)}, u32[]{:S(2)}, u32[]{:S(2)}) async-start(bf16[48,32,512]{2,0,1:T(8,128)(2,1)} %bitcast.12), calls=%async_computation | async-start | bytes 3145728 | tf_op jit(solution)/shard_map/all_to_all | solution.py:192
  32.6 13.3 %collective-permute-start = (bf16[256,512]{1,0:T(8,128)(2,1)S(1)}, bf16[256,512]{1,0:T(8,128)(2,1)S(1)}, u32[]{:S(2)}, u32[]{:S(2)}) collective-permute-start(bf16[256,512]{1,0:T(8,128)(2,1)S(1)} %slice.8), channel_id=1, source_target_pairs={{0,32},{32,64},{64,96},{96,128},{128,160},{160,192},{192,224},{1,3... | collective-permute-start | bytes 786440 | tf_op jit(solution)/shard_map/ppermute | solution.py:35
  41.4 7.6 %copy-start = (f32[1280,512]{1,0:T(8,128)}, f32[1280,512]{1,0:T(8,128)S(1)}, u32[]{:S(2)}) copy-start(f32[1280,512]{1,0:T(8,128)S(1)} %get-tuple-element.24.running) | copy-start | bytes 7864324
  41.4 7.6 %copy-start.2 = (f32[1152,512]{1,0:T(8,128)}, f32[1152,512]{1,0:T(8,128)S(1)}, u32[]{:S(2)}) copy-start(f32[1152,512]{1,0:T(8,128)S(1)} %get-tuple-element.30.upper) | copy-start | bytes 7077892
  41.4 15.3 %collective-permute-start.1 = (bf16[128,512]{1,0:T(8,128)(2,1)}, bf16[128,512]{1,0:T(8,128)(2,1)}, u32[]{:S(2)}, u32[]{:S(2)}) collective-permute-start(bf16[128,512]{1,0:T(8,128)(2,1)} %get-tuple-element.26), channel_id=1, source_target_pairs={{0,32},{32,64},{64,96},{96,128},{128,160},{160,192},{192,224},{1,3... | collective-permute-start | bytes 393224 | tf_op jit(solution)/shard_map/ppermute | solution.py:35
  46.0 0.7 copy-start.6
  46.7 0.9 %copy-start.7 = (bf16[256,512]{1,0:T(8,128)(2,1)S(1)}, bf16[256,512]{1,0:T(8,128)(2,1)}, u32[]{:S(2)}) copy-start(bf16[256,512]{1,0:T(8,128)(2,1)} %copy-done.6) | copy-start | bytes 786436
  47.6 17.1 %copy-start.10 = (f32[512]{0:T(512)S(1)}, f32[512]{0:T(512)}, u32[]{:S(2)}) copy-start(f32[512]{0:T(512)} %param.14) | copy-start | bytes 6148
  49.1 0.8 %copy-start.4 = (f32[256,512]{1,0:T(8,128)}, f32[256,512]{1,0:T(8,128)S(1)}, u32[]{:S(2)}) copy-start(f32[256,512]{1,0:T(8,128)S(1)} %get-tuple-element.29.upper12) | copy-start | bytes 1572868
  49.9 0.6 copy-start.8
  50.5 14.2 %all-to-all-start.1 = ((f32[8,2,512]{2,1,0:T(2,128)}), f32[8,2,512]{2,1,0:T(2,128)S(1)}, u32[]{:S(2)}, u32[]{:S(2)}) async-start(f32[8,2,512]{2,1,0:T(2,128)} %get-tuple-element.25), calls=%async_computation.1 | async-start | bytes 65536 | tf_op jit(solution)/shard_map/all_to_all | solution.py:243
  64.7 1.7 %copy-start.1 = (f32[1280,512]{1,0:T(8,128)S(1)}, f32[1280,512]{1,0:T(8,128)}, u32[]{:S(2)}) copy-start(f32[1280,512]{1,0:T(8,128)} %copy-done) | copy-start | bytes 7864324
  66.5 1.7 %copy-start.3 = (f32[1152,512]{1,0:T(8,128)S(1)}, f32[1152,512]{1,0:T(8,128)}, u32[]{:S(2)}) copy-start(f32[1152,512]{1,0:T(8,128)} %copy-done.2) | copy-start | bytes 7077892
  68.2 1.0 %copy-start.5 = (f32[256,512]{1,0:T(8,128)S(1)}, f32[256,512]{1,0:T(8,128)}, u32[]{:S(2)}) copy-start(f32[256,512]{1,0:T(8,128)} %copy-done.4) | copy-start | bytes 1572868
  69.2 0.9 %copy-start.9 = (bf16[128,512]{1,0:T(8,128)(2,1)S(1)}, bf16[128,512]{1,0:T(8,128)(2,1)}, u32[]{:S(2)}) copy-start(bf16[128,512]{1,0:T(8,128)(2,1)} %copy-done.8) | copy-start | bytes 393220

commit v2 on v0

v2 whole, which is shorter than its diff:
```python
import functools

import jax
import jax.numpy as jnp
from jax import lax
from jax.experimental import pallas as pl
from jax.experimental.pallas import tpu as pltpu
from jax.sharding import PartitionSpec as P

BLOCK = 128
SUB = 64
VMEM = pl.BlockSpec(memory_space=pltpu.VMEM)
SMEM = pl.BlockSpec(memory_space=pltpu.SMEM)
ANY = pl.BlockSpec(memory_space=pl.ANY)
HBM = pl.BlockSpec(memory_space=pltpu.HBM)


def dot(a, b):
    return jnp.dot(a, b, preferred_element_type=jnp.float32)


def call(kernel, out_shape, in_specs, out_specs=None, scratch=(), limit=24):
    if out_specs is None:
        out_specs = jax.tree.map(lambda _: VMEM, out_shape)
    return pl.pallas_call(
        kernel,
        out_shape=out_shape,
        in_specs=in_specs,
        out_specs=out_specs,
        scratch_shapes=scratch,
        compiler_params=pltpu.CompilerParams(vmem_limit_bytes=limit * 1024 * 1024),
    )


def from_behind(value, axis):
    count = lax.axis_size(axis)
    return lax.ppermute(value, axis, [(source, source + 1) for source in range(count - 1)])


def regroup_kernel(raw, out, held, sems):
    groups, _, cols = out.shape
    count = sems.shape[0]
    each = groups // count
    copies = []
    for c in range(count):
        part = pl.ds(c * each * cols, each * cols)
        copies.append(pltpu.make_async_copy(raw.at[:, part], held.at[:, part], sems.at[c]))
    for copy in copies:
        copy.start()
    for c, copy in enumerate(copies):
        copy.wait()
        for k in range(c * each, (c + 1) * each):
            out[k] = held[:, k * cols : (k + 1) * cols]


def prepare_kernel(
    band_taps, real_taps, imag_taps, short_taps, keep_log, gap_gain,
    band_ref, pair_ref, short_ref, sums_ref, scale, gain_scale, ends,
):
    def toeplitz(taps):
        row = jnp.concatenate([taps[...].astype(jnp.float32), jnp.zeros((1, BLOCK))], axis=1)
        rows = pltpu.roll(
            jnp.broadcast_to(row, (2 * BLOCK, 2 * BLOCK)), BLOCK, 1, stride=1, stride_axis=0
        )
        return rows[:, :BLOCK].T.astype(jnp.bfloat16)

    band_ref[...] = toeplitz(band_taps)
    pair_ref[:BLOCK, :] = toeplitz(real_taps)
    pair_ref[BLOCK:, :] = toeplitz(imag_taps)
    short_ref[...] = toeplitz(short_taps)
    row = lax.broadcasted_iota(jnp.int32, (BLOCK, 2 * BLOCK), 0)
    col = lax.broadcasted_iota(jnp.int32, (BLOCK, 2 * BLOCK), 1) % BLOCK
    keep = (col <= row) & (col // SUB == row // SUB)
    sums_ref[...] = jnp.where(keep, 1.0, 0.0).astype(jnp.bfloat16)
    offset = (lax.broadcasted_iota(jnp.int32, scale.shape, 0) + 1).astype(jnp.float32)
    scale[...] = jnp.exp(-offset * keep_log[...])
    gain = gap_gain[...]
    place = lax.broadcasted_iota(jnp.int32, gain.shape, 1) % SUB
    reach = 1
    while reach < SUB:
        gain = gain * jnp.where(place >= reach, pltpu.roll(gain, reach, 1), 1.0)
        reach *= 2
    inverse = 1.0 / gain
    whole = jnp.exp(SUB * keep_log[...])
    for b in range(gain.shape[0]):
        column = jnp.broadcast_to(inverse[b : b + 1, :], (BLOCK, BLOCK)).T
        gain_scale[block(b), :] = column
        for h in range(BLOCK // SUB):
            s = b * (BLOCK // SUB) + h
            last = column[(h + 1) * SUB - 1 : (h + 1) * SUB, :]
            lanes = jnp.concatenate([1.0 / last] * (ends.shape[1] // BLOCK), axis=1)
            ends[s : s + 1, :] = whole * lanes


def energy_of(pair, window):
    both = dot(pair, window)
    real, imag = both[:BLOCK], both[BLOCK:]
    return (real * real + imag * imag).astype(jnp.bfloat16)


def inverse_decay(scale, gain_scale):
    cols = scale.shape[1]
    lanes = jnp.concatenate([gain_scale] * (cols // 128), axis=1)
    return jnp.concatenate([scale] * (BLOCK // SUB), axis=0) * lanes


def scaled_energy(energy, rate, scale, gain_scale):
    return energy.astype(jnp.float32) * (inverse_decay(scale, gain_scale) * rate)


def last_sums(scaled):
    return [
        jnp.sum(scaled[h * SUB : (h + 1) * SUB, :], axis=0, keepdims=True)
        for h in range(BLOCK // SUB)
    ]


def block(b, n=1):
    return pl.ds(b * BLOCK, n * BLOCK)


def main_kernel(
    count, signal, band_m, pair_m, rate, scale, gain_scale, band1, energy, energy_last, tails, band
):
    for b in range(1, count):
        band[block(b), :] = dot(band_m[...], signal[block(b - 1, 2), :]).astype(jnp.bfloat16)
    band1[...] = band[block(1), :]
    for b in range(2, count):
        e = energy_of(pair_m[...], band[block(b - 1, 2), :])
        energy[block(b - 2), :] = e
        if b == count - 1:
            energy_last[...] = e
        sums = last_sums(scaled_energy(e, rate[...], scale[...], gain_scale[block(b), :]))
        for h, row in enumerate(sums):
            at = (b - 2) * len(sums) + h
            tails[at : at + 1, :] = row


def edge_kernel(
    subs, prior_any, signal, band1, tails, band_m, pair_m, rate, scale, gain_scale, ends,
    energy, totals, window, sem,
):
    copy = pltpu.make_async_copy(prior_any, window.at[block(0, 2), :], sem)
    copy.start()
    window[block(2), :] = signal[block(0), :]
    copy.wait()
    band = [
        dot(band_m[...], window[block(b, 2), :]).astype(jnp.bfloat16) for b in range(2)
    ] + [band1[...]]
    rows = []
    for b in range(2):
        e = energy_of(pair_m[...], jnp.concatenate([band[b], band[b + 1]], axis=0))
        energy[block(b), :] = e
        rows += last_sums(scaled_energy(e, rate[...], scale[...], gain_scale[block(b), :]))
    edge = len(rows)
    value = jnp.zeros_like(ends[0:1, :])
    decay = jnp.ones_like(value)
    for s in range(subs):
        end = rows[s] if s < edge else tails[s - edge : s - edge + 1, :]
        step = ends[s : s + 1, :]
        value = step * (value + end)
        decay = decay * step
    both = jnp.concatenate([decay, value], axis=0)
    for k in range(totals.shape[0]):
        totals[k] = both


def ratio_kernel(
    count, position, totals, start, before, head, rest, short_m, sums_m, rate, scale, gain_scale,
    ends, out, buffer, sems,
):
    parts = sems.shape[0]
    each = count // parts
    state = start[...]
    for k in range(totals.shape[0]):
        new = totals[k, 0:1, :] * state + totals[k, 1:2, :]
        state = jnp.where(k < position[0], new, state)

    def energy(b):
        return before[...] if b < 0 else head[block(b), :] if b < 2 else rest[block(b - 2), :]

    sends = []
    for b in range(count):
        current = energy(b)
        inverse = inverse_decay(scale[...], gain_scale[block(b), :])
        scaled = current.astype(jnp.float32) * (inverse * rate[...])
        high = scaled.astype(jnp.bfloat16)
        low = (scaled - high.astype(jnp.float32)).astype(jnp.bfloat16)
        running = dot(sums_m[...], jnp.concatenate([high, low], axis=0))
        window = rest[block(b - 3, 2), :] if b > 2 else jnp.concatenate([energy(b - 1), current], axis=0)
        upper = dot(short_m[...], window) * inverse
        for h in range(BLOCK // SUB):
            at = b * BLOCK + h * SUB
            run = running[h * SUB : (h + 1) * SUB, :]
            buffer[at : at + SUB, :] = upper[h * SUB : (h + 1) * SUB, :] / (run + state)
            s = at // SUB
            state = ends[s : s + 1, :] * (state + run[SUB - 1 : SUB, :])
        if (b + 1) % each == 0:
            c = b // each
            part = block(c * each, each)
            copy = pltpu.make_async_copy(buffer.at[part, :], out.at[part, :], sems.at[c])
            copy.start()
            sends.append(copy)
    for copy in sends:
        copy.wait()


def body(raw, band_taps, real_taps, imag_taps, short_taps, lta_rate, lta_start, gap_gain):
    f32, bf16 = jnp.float32, jnp.bfloat16
    struct = jax.ShapeDtypeStruct
    hbm = lambda x: pltpu.with_memory_space_constraint(x, pltpu.HBM)
    parts, groups = lax.axis_size("chan"), lax.axis_size("tm")
    held, cols = raw.shape[0], raw.shape[1] // parts
    total = held * parts
    count, subs = total // BLOCK, total // SUB
    grouped = call(
        regroup_kernel,
        pltpu.VMEM((parts, held, cols), bf16),
        [HBM],
        out_specs=VMEM,
        scratch=[pltpu.VMEM(raw.shape, bf16), pltpu.SemaphoreType.DMA((min(16, parts),))],
    )(hbm(raw))
    signal = lax.all_to_all(grouped, "chan", split_axis=0, concat_axis=0, tiled=True)
    signal = signal.reshape(total, cols)

    given = (band_taps, real_taps, imag_taps, short_taps, lta_rate, gap_gain)
    signal, given = lax.optimization_barrier((signal, given))
    band_taps, real_taps, imag_taps, short_taps, lta_rate, gap_gain = given
    taps = [x.reshape(1, BLOCK) for x in (band_taps, real_taps, imag_taps, short_taps)]
    keep_log = jnp.log1p(-(1.0 - (1.0 - lta_rate))).reshape(1, cols)
    rate = lta_rate.reshape(1, cols)
    matrix = struct((BLOCK, 2 * BLOCK), bf16)
    band_m, pair_m, short_m, sums_m, scale, gain_scale, ends = call(
        prepare_kernel,
        [
            matrix,
            struct((2 * BLOCK, 2 * BLOCK), bf16),
            matrix,
            matrix,
            struct((SUB, cols), f32),
            struct((total, 128), f32),
            struct((subs, cols), f32),
        ],
        [VMEM] * 6,
    )(*taps, keep_log, gap_gain.reshape(count, BLOCK))

    prior = from_behind(signal[total - 2 * BLOCK :], "tm")
    band1, rest, energy_last, tails = call(
        functools.partial(main_kernel, count),
        [
            struct((BLOCK, cols), bf16),
            struct((total - 2 * BLOCK, cols), bf16),
            struct((BLOCK, cols), bf16),
            struct((subs - 2 * BLOCK // SUB, cols), f32),
        ],
        [VMEM] * 6,
        scratch=[pltpu.VMEM((total, cols), bf16)],
    )(signal, band_m, pair_m, rate, scale, gain_scale)
    energy_before = from_behind(energy_last, "tm")
    head, totals = call(
        functools.partial(edge_kernel, subs),
        [struct((2 * BLOCK, cols), bf16), pltpu.VMEM((groups, 2, cols), f32)],
        [ANY] + [VMEM] * 9,
        scratch=[pltpu.VMEM((3 * BLOCK, cols), bf16), pltpu.SemaphoreType.DMA],
    )(prior, signal, band1, tails, band_m, pair_m, rate, scale, gain_scale, ends)
    totals = lax.all_to_all(totals, "tm", split_axis=0, concat_axis=0, tiled=True)
    position = lax.axis_index("tm").astype(jnp.int32).reshape(1)
    return call(
        functools.partial(ratio_kernel, count),
        pltpu.HBM((total, cols), f32),
        [SMEM] + [VMEM] * 11,
        out_specs=HBM,
        scratch=[pltpu.VMEM((total, cols), f32), pltpu.SemaphoreType.DMA((4,))],
    )(position, totals, lta_start.reshape(1, cols), energy_before, head, rest, short_m, sums_m, rate,
      scale, gain_scale, ends)


def solution(mesh):
    return jax.shard_map(
        body,
        mesh=mesh,
        in_specs=(P(("tm", "chan"), None), P(), P(), P(), P(), P("chan"), P("chan"), P("tm")),
        out_specs=P("tm", "chan"),
        check_vma=False,
    )
```

time: 123 us -> 63.9 us (0.52)
  other arithmetic: 24.7 us -> 0.01 us
  blocking collectives: 47 us -> 29.3 us
  matrix products: 13.4 us -> 0 us
  local copies, waits for them, and re-layouts: 11.9 us -> 0.06 us
  Pallas kernels: 0 us -> 8.06 us
  waiting for transfers between devices: 4.06 us -> 8.03 us
  starting transfers between devices: 20.5 us -> 18 us
    all_gather x2 -> x0, blocking collectives: 47 us -> none  [prefix(): everything = jax.tree.map(lambda part: lax.all_gather(part, axis), x)]
    all_to_all x0 -> x1, blocking collectives: none -> 29.3 us  [body(): lax.all_to_all(grouped, 'chan', split_axis=0, concat_axis=0, tiled=True)]
    reduce_sum x1 -> x0, other arithmetic: 23.5 us -> none  [band_matrices(): jnp.sum(jnp.where(lag[:, :, None] == picks[None, None, :], weights, 0.0),...]
    dot_general x9 -> x0, matrix products: 13.4 us -> none  [the longest x4 6.79 us: block_filter(): jnp.einsum('ij,bjc->bic', earlier, prior, preferred_element_type=jnp.floa...]
    pallas_call x0 -> x5, Pallas kernels: none -> 8.06 us  [the longest x1 2.77 us: body(): call(functools.partial(ratio_kernel, count), pltpu.HBM((total, cols), f32...]
    all_to_all x1, waiting for transfers between devices: 0.01 us -> 8.02 us  [body(): lax.all_to_all(totals, 'tm', split_axis=0, concat_axis=0, tiled=True)]
    ppermute x3 -> x2, starting transfers between devices: 12.9 us -> 7.67 us  [from_behind(): lax.ppermute(value, axis, [(source, source + 1) for source in range(count...]
    ppermute x3 -> x2, waiting for transfers between devices: 4.05 us -> 0.01 us  [from_behind(): lax.ppermute(value, axis, [(source, source + 1) for source in range(count...]
  transfers between devices with their start and end apart: 4 -> 3, of which waited for: 2 -> 1; matrix products, arithmetic and copies ran while one was open for 26% -> 0% of each run, Pallas kernels for 0% -> 6%
where the time goes in v2:
time: 63.9 us; the launch traced here: 63.6 us
  blocking collectives  29.3 us (46%)
  starting transfers between devices  18 us (28%)
  Pallas kernels  8.06 us (13%)
  waiting for transfers between devices  8.03 us (13%)
    all_to_all x1, blocking collectives, body(): lax.all_to_all(grouped, 'chan', split_axis=0, concat_axis=0, tiled=True)  29.3 us
    all_to_all x1, starting transfers between devices, body(): lax.all_to_all(totals, 'tm', split_axis=0, concat_axis=0, tiled=True)  10.3 us
    all_to_all x1, waiting for transfers between devices, body(): lax.all_to_all(totals, 'tm', split_axis=0, concat_axis=0, tiled=True)  8.02 us
    ppermute x2, starting transfers between devices, from_behind(): lax.ppermute(value, axis, [(source, source + 1) for source in range(count...  7.67 us
    pallas_call x1, Pallas kernels, body(): call(functools.partial(ratio_kernel, count), pltpu.HBM((total, cols), f32...  2.77 us
    pallas_call x1, Pallas kernels, body(): call(regroup_kernel, pltpu.VMEM((parts, held, cols), bf16), [HBM], out_sp...  1.6 us
    pallas_call x1, Pallas kernels, body(): call(functools.partial(main_kernel, count), [struct((BLOCK, cols), bf16),...  1.58 us
  transfers between devices with their start and end apart: 3, of which 1 were waited for; matrix products, arithmetic and copies ran while one was open for 0% of the time, Pallas kernels for 6%

profile of v2, /device:TPU:2, one launch (start us, length us, event | category | flops | bytes accessed | tf_op | source)
XLA Modules:
  0.0 63.6 jit_solution(5787805894483910532)
XLA Ops:
  0.0 1.6 %shard_map.82 = bf16[32,48,512]{2,1,0:T(8,128)(2,1)S(1)} custom-call(bf16[48,16384]{1,0:T(8,128)(2,1)} %raw.1), custom_call_target="tpu_custom_call" | custom-call | tf_op jit(solution)/shard_map/pallas_call | solution.py:216
  1.6 0.0 copy-start
  1.6 0.0 copy-start.1
  1.6 0.0 copy-start.3
  1.6 0.0 copy-start.4
  1.7 0.0 copy-start.5
  1.7 0.0 copy-start.6
  1.7 29.3 %all_to_all.10 = bf16[32,48,512]{2,1,0:T(8,128)(2,1)S(1)} all-to-all(bf16[32,48,512]{2,1,0:T(8,128)(2,1)S(1)} %shard_map.82), channel_id=1, replica_groups=mesh['tm'=8,'chan'=32] {'chan'}, dimensions={0} | all-to-all | bytes 3145728 | tf_op jit(solution)/shard_map/all_to_all | solution.py:223
  31.0 3.9 %collective-permute-start = (bf16[256,512]{1,0:T(8,128)(2,1)S(1)}, bf16[256,512]{1,0:T(8,128)(2,1)S(1)}, u32[]{:S(2)}, u32[]{:S(2)}) collective-permute-start(bf16[256,512]{1,0:T(8,128)(2,1)S(1)} %slice.3), channel_id=1, source_target_pairs={{0,32},{32,64},{64,96},{96,128},{128,160},{160,192},{192,224},{1,3... | collective-permute-start | bytes 786440 | tf_op jit(solution)/shard_map/ppermute | solution.py:37
  34.8 0.0 copy-done
  34.9 0.0 copy-done.1
  34.9 0.0 copy-done.3
  34.9 0.0 copy-done.4
  34.9 0.0 copy-done.5
  34.9 0.0 copy-done.6
  34.9 0.8 %shard_map.83 = (bf16[128,256]{1,0:T(8,128)(2,1)S(1)}, bf16[256,256]{1,0:T(8,128)(2,1)S(1)}, bf16[128,256]{1,0:T(8,128)(2,1)S(1)}, bf16[128,256]{1,0:T(8,128)(2,...) custom-call(bf16[1,128]{1,0:T(2,128)(2,1)S(1)} %bitcast.19, ...), custom_call_target="tpu_custom_call" | custom-call | tf_op jit(solution)/shard_map/pallas_call | solution.py:233
  35.8 1.6 %shard_map.84 = (bf16[128,512]{1,0:T(8,128)(2,1)S(1)}, bf16[1280,512]{1,0:T(8,128)(2,1)S(1)}, bf16[128,512]{1,0:T(8,128)(2,1)S(1)}, f32[20,512]{1,0:T(8,128)S(1)}) custom-call(bf16[1536,512]{1,0:T(8,128)(2,1)S(1)} %bitcast.11, bf16[128,256]{1,0:T(8,128)(2,1)S(1)} %get-tuple-element.32.band_m, bf16[256,256]{1,0:T(8,128)(2,1)S(1)} %get-tuple-element.33.pair_m, ...), custom_call_target="tpu_custom_call" | custom-call | tf_op jit(solution)/shard_map/pallas_call | solution.py:248
  37.4 3.8 %collective-permute-start.1 = (bf16[128,512]{1,0:T(8,128)(2,1)S(1)}, bf16[128,512]{1,0:T(8,128)(2,1)S(1)}, u32[]{:S(2)}, u32[]{:S(2)}) collective-permute-start(bf16[128,512]{1,0:T(8,128)(2,1)S(1)} %get-tuple-element.40), channel_id=1, source_target_pairs={{0,32},{32,64},{64,96},{96,128},{128,160},{160,192},{192,224},{1,3... | collective-permute-start | bytes 393224 | tf_op jit(solution)/shard_map/ppermute | solution.py:37
  41.2 0.0 collective-permute-done.prior_any
  41.2 0.0 copy-start.2
  41.2 1.3 %shard_map.85 = (bf16[256,512]{1,0:T(8,128)(2,1)S(1)}, f32[8,2,512]{2,1,0:T(2,128)}) custom-call(bf16[256,512]{1,0:T(8,128)(2,1)S(1)} %collective-permute-done.prior_any, bf16[1536,512]{1,0:T(8,128)(2,1)S(1)} %bitcast.12, bf16[128,512]{1,0:T(8,128)(2,1)S(1)} %get-tuple-element.36.band1, f32[20,512]{1,0:T(8,128)S(1)} %get-tuple-element.37.tails, ...), custom_call_target="tpu_custom_call" | custom-call | tf_op jit(solution)/shard_map/pallas_call | solution.py:260
  42.5 10.3 %all-to-all-start.1 = ((f32[8,2,512]{2,1,0:T(2,128)}), f32[8,2,512]{2,1,0:T(2,128)S(1)}, u32[]{:S(2)}, u32[]{:S(2)}) async-start(f32[8,2,512]{2,1,0:T(2,128)} %get-tuple-element.39), calls=%async_computation.1 | async-start | bytes 65536 | tf_op jit(solution)/shard_map/all_to_all | solution.py:266
  52.8 0.0 collective-permute-done.1.before
  52.8 8.0 %all-to-all-done.1.totals = f32[8,2,512]{2,1,0:T(2,128)S(1)} async-done(((f32[8,2,512]{2,1,0:T(2,128)}), f32[8,2,512]{2,1,0:T(2,128)S(1)}, u32[]{:S(2)}, u32[]{:S(2)}) %all-to-all-start.1) | async-done | bytes 32800 | tf_op jit(solution)/shard_map/all_to_all | solution.py:266
  60.8 0.0 copy-done.2
  60.8 2.8 %shard_map.86 = f32[1536,512]{1,0:T(8,128)} custom-call(s32[1]{0:T(128)} %bitcast.position, f32[8,2,512]{2,1,0:T(2,128)S(1)} %all-to-all-done.1.totals, f32[1,512]{1,0:T(1,128)S(1)} %bitcast.18, bf16[128,512]{1,0:T(8,128)(2,1)S(1)} %collective-permute-done.1.before, bf16[256,512]{1,0:T(8,128)(2,1)S(1)} %get-tuple-element.41.head, ...), custom_call_target="tpu_custom_call" | custom-call | tf_op jit(solution)/shard_map/pallas_call | solution.py:268
  (2 shorter events, 0.0 us)
Async XLA Ops:
  1.6 33.2 %copy-start = (f32[512]{0:T(512)S(1)}, f32[512]{0:T(512)}, u32[]{:S(2)}) copy-start(f32[512]{0:T(512)} %param.13) | copy-start | bytes 6148
  1.6 33.3 %copy-start.1 = (f32[1536]{0:T(1024)S(1)}, f32[1536]{0:T(1024)}, u32[]{:S(2)}) copy-start(f32[1536]{0:T(1024)} %param.15) | copy-start | bytes 18436
  1.6 33.2 %copy-start.3 = (bf16[128]{0:T(256)(128)(2,1)S(1)}, bf16[128]{0:T(256)(128)(2,1)}, u32[]{:S(2)}) copy-start(bf16[128]{0:T(256)(128)(2,1)} %param.9) | copy-start | bytes 772
  1.6 33.2 %copy-start.4 = (bf16[128]{0:T(256)(128)(2,1)S(1)}, bf16[128]{0:T(256)(128)(2,1)}, u32[]{:S(2)}) copy-start(bf16[128]{0:T(256)(128)(2,1)} %param.10) | copy-start | bytes 772
  1.7 33.2 %copy-start.5 = (bf16[128]{0:T(256)(128)(2,1)S(1)}, bf16[128]{0:T(256)(128)(2,1)}, u32[]{:S(2)}) copy-start(bf16[128]{0:T(256)(128)(2,1)} %param.11) | copy-start | bytes 772
  1.7 33.2 %copy-start.6 = (bf16[128]{0:T(256)(128)(2,1)S(1)}, bf16[128]{0:T(256)(128)(2,1)}, u32[]{:S(2)}) copy-start(bf16[128]{0:T(256)(128)(2,1)} %param.12) | copy-start | bytes 772
  31.0 10.2 %collective-permute-start = (bf16[256,512]{1,0:T(8,128)(2,1)S(1)}, bf16[256,512]{1,0:T(8,128)(2,1)S(1)}, u32[]{:S(2)}, u32[]{:S(2)}) collective-permute-start(bf16[256,512]{1,0:T(8,128)(2,1)S(1)} %slice.3), channel_id=1, source_target_pairs={{0,32},{32,64},{64,96},{96,128},{128,160},{160,192},{192,224},{1,3... | collective-permute-start | bytes 786440 | tf_op jit(solution)/shard_map/ppermute | solution.py:37
  37.4 15.5 %collective-permute-start.1 = (bf16[128,512]{1,0:T(8,128)(2,1)S(1)}, bf16[128,512]{1,0:T(8,128)(2,1)S(1)}, u32[]{:S(2)}, u32[]{:S(2)}) collective-permute-start(bf16[128,512]{1,0:T(8,128)(2,1)S(1)} %get-tuple-element.40), channel_id=1, source_target_pairs={{0,32},{32,64},{64,96},{96,128},{128,160},{160,192},{192,224},{1,3... | collective-permute-start | bytes 393224 | tf_op jit(solution)/shard_map/ppermute | solution.py:37
  41.2 19.7 %copy-start.2 = (f32[512]{0:T(512)S(1)}, f32[512]{0:T(512)}, u32[]{:S(2)}) copy-start(f32[512]{0:T(512)} %param.14) | copy-start | bytes 6148
  42.5 18.4 %all-to-all-start.1 = ((f32[8,2,512]{2,1,0:T(2,128)}), f32[8,2,512]{2,1,0:T(2,128)S(1)}, u32[]{:S(2)}, u32[]{:S(2)}) async-start(f32[8,2,512]{2,1,0:T(2,128)} %get-tuple-element.39), calls=%async_computation.1 | async-start | bytes 65536 | tf_op jit(solution)/shard_map/all_to_all | solution.py:266

commit v3 on v2

--- a/solution.py
+++ b/solution.py
@@ -38,19 +38,20 @@
 
 
 def regroup_kernel(raw, out, held, sems):
-    groups, _, cols = out.shape
+    groups, rows, cols = out.shape
     count = sems.shape[0]
-    each = groups // count
+    each = rows // count
     copies = []
     for c in range(count):
-        part = pl.ds(c * each * cols, each * cols)
-        copies.append(pltpu.make_async_copy(raw.at[:, part], held.at[:, part], sems.at[c]))
+        part = pl.ds(c * each, each)
+        copies.append(pltpu.make_async_copy(raw.at[part, :], held.at[part, :], sems.at[c]))
     for copy in copies:
         copy.start()
     for c, copy in enumerate(copies):
         copy.wait()
-        for k in range(c * each, (c + 1) * each):
-            out[k] = held[:, k * cols : (k + 1) * cols]
+        part = pl.ds(c * each, each)
+        for k in range(groups):
+            out[k, part, :] = held[part, k * cols : (k + 1) * cols]
 
 
 def prepare_kernel(
@@ -92,6 +93,10 @@
             ends[s : s + 1, :] = whole * lanes
 
 
+def halo_kernel(signal, halo):
+    halo[...] = signal[signal.shape[0] - halo.shape[0] :, :]
+
+
 def energy_of(pair, window):
     both = dot(pair, window)
     real, imag = both[:BLOCK], both[BLOCK:]
@@ -120,28 +125,47 @@
 
 
 def main_kernel(
-    count, signal, band_m, pair_m, rate, scale, gain_scale, band1, energy, energy_last, tails, band
+    count, signal, band_m, pair_m, rate, scale, gain_scale, band1, energy, energy_last, tails, band,
+    energy_v, tails_v, sems,
 ):
     for b in range(1, count):
         band[block(b), :] = dot(band_m[...], signal[block(b - 1, 2), :]).astype(jnp.bfloat16)
     band1[...] = band[block(1), :]
-    for b in range(2, count):
+    order = [count - 1, *range(2, count - 1)]
+    half = len(order) // 2
+    copies = []
+
+    def send(source, target):
+        copy = pltpu.make_async_copy(source, target, sems.at[len(copies)])
+        copy.start()
+        copies.append(copy)
+
+    for done, b in enumerate(order):
         e = energy_of(pair_m[...], band[block(b - 1, 2), :])
-        energy[block(b - 2), :] = e
-        if b == count - 1:
-            energy_last[...] = e
+        energy_v[block(b - 2), :] = e
         sums = last_sums(scaled_energy(e, rate[...], scale[...], gain_scale[block(b), :]))
         for h, row in enumerate(sums):
             at = (b - 2) * len(sums) + h
-            tails[at : at + 1, :] = row
+            tails_v[at : at + 1, :] = row
+        if done == 0:
+            send(energy_v.at[block(count - 3), :], energy_last)
+        if done == half:
+            send(energy_v.at[block(0, half), :], energy.at[block(0, half), :])
+    send(tails_v, tails)
+    part = block(half, count - 2 - half)
+    send(energy_v.at[part, :], energy.at[part, :])
+    for copy in copies:
+        copy.wait()
 
 
 def edge_kernel(
-    subs, prior_any, signal, band1, tails, band_m, pair_m, rate, scale, gain_scale, ends,
-    energy, totals, window, sem,
+    subs, prior_any, signal, band1, tails_hbm, band_m, pair_m, rate, scale, gain_scale, ends,
+    energy, totals, window, tails, sems,
 ):
-    copy = pltpu.make_async_copy(prior_any, window.at[block(0, 2), :], sem)
+    copy = pltpu.make_async_copy(prior_any, window.at[block(0, 2), :], sems.at[0])
     copy.start()
+    fetch = pltpu.make_async_copy(tails_hbm, tails, sems.at[1])
+    fetch.start()
     window[block(2), :] = signal[block(0), :]
     copy.wait()
     band = [
@@ -153,6 +177,7 @@
         energy[block(b), :] = e
         rows += last_sums(scaled_energy(e, rate[...], scale[...], gain_scale[block(b), :]))
     edge = len(rows)
+    fetch.wait()
     value = jnp.zeros_like(ends[0:1, :])
     decay = jnp.ones_like(value)
     for s in range(subs):
@@ -165,16 +190,21 @@
         totals[k] = both
 
 
+def carry_kernel(position, totals, start, carry):
+    state = start[...]
+    for k in range(totals.shape[0]):
+        new = totals[k, 0:1, :] * state + totals[k, 1:2, :]
+        state = jnp.where(k < position[0], new, state)
+    carry[...] = state
+
+
 def ratio_kernel(
-    count, position, totals, start, before, head, rest, short_m, sums_m, rate, scale, gain_scale,
+    count, carry, before, head, rest, short_m, sums_m, rate, scale, gain_scale,
     ends, out, buffer, sems,
 ):
     parts = sems.shape[0]
     each = count // parts
-    state = start[...]
-    for k in range(totals.shape[0]):
-        new = totals[k, 0:1, :] * state + totals[k, 1:2, :]
-        state = jnp.where(k < position[0], new, state)
+    state = carry[...]
 
     def energy(b):
         return before[...] if b < 0 else head[block(b), :] if b < 2 else rest[block(b - 2), :]
@@ -218,7 +248,7 @@
         pltpu.VMEM((parts, held, cols), bf16),
         [HBM],
         out_specs=VMEM,
-        scratch=[pltpu.VMEM(raw.shape, bf16), pltpu.SemaphoreType.DMA((min(16, parts),))],
+        scratch=[pltpu.VMEM(raw.shape, bf16), pltpu.SemaphoreType.DMA((3,))],
     )(hbm(raw))
     signal = lax.all_to_all(grouped, "chan", split_axis=0, concat_axis=0, tiled=True)
     signal = signal.reshape(total, cols)
@@ -244,34 +274,51 @@
         [VMEM] * 6,
     )(*taps, keep_log, gap_gain.reshape(count, BLOCK))
 
-    prior = from_behind(signal[total - 2 * BLOCK :], "tm")
+    halo = call(halo_kernel, pltpu.VMEM((2 * BLOCK, cols), bf16), [VMEM])(signal)
+    prior = from_behind(halo, "tm")
     band1, rest, energy_last, tails = call(
         functools.partial(main_kernel, count),
         [
             struct((BLOCK, cols), bf16),
-            struct((total - 2 * BLOCK, cols), bf16),
-            struct((BLOCK, cols), bf16),
-            struct((subs - 2 * BLOCK // SUB, cols), f32),
+            pltpu.HBM((total - 2 * BLOCK, cols), bf16),
+            pltpu.HBM((BLOCK, cols), bf16),
+            pltpu.HBM((subs - 2 * BLOCK // SUB, cols), f32),
         ],
         [VMEM] * 6,
-        scratch=[pltpu.VMEM((total, cols), bf16)],
+        out_specs=[VMEM, HBM, HBM, HBM],
+        scratch=[
+            pltpu.VMEM((total, cols), bf16),
+            pltpu.VMEM((total - 2 * BLOCK, cols), bf16),
+            pltpu.VMEM((subs - 2 * BLOCK // SUB, cols), f32),
+            pltpu.SemaphoreType.DMA((4,)),
+        ],
     )(signal, band_m, pair_m, rate, scale, gain_scale)
     energy_before = from_behind(energy_last, "tm")
     head, totals = call(
         functools.partial(edge_kernel, subs),
         [struct((2 * BLOCK, cols), bf16), pltpu.VMEM((groups, 2, cols), f32)],
-        [ANY] + [VMEM] * 9,
-        scratch=[pltpu.VMEM((3 * BLOCK, cols), bf16), pltpu.SemaphoreType.DMA],
-    )(prior, signal, band1, tails, band_m, pair_m, rate, scale, gain_scale, ends)
+        [ANY] + [VMEM] * 2 + [HBM] + [VMEM] * 6,
+        scratch=[
+            pltpu.VMEM((3 * BLOCK, cols), bf16),
+            pltpu.VMEM((subs - 2 * BLOCK // SUB, cols), f32),
+            pltpu.SemaphoreType.DMA((2,)),
+        ],
+    )(prior, signal, band1, hbm(tails), band_m, pair_m, rate, scale, gain_scale, ends)
+    position = lax.axis_index("tm").astype(jnp.int32).reshape(1)
+    totals, position, start = lax.optimization_barrier(
+        (totals, position, lta_start.reshape(1, cols))
+    )
     totals = lax.all_to_all(totals, "tm", split_axis=0, concat_axis=0, tiled=True)
-    position = lax.axis_index("tm").astype(jnp.int32).reshape(1)
+    carry = call(
+        carry_kernel, struct((1, cols), f32), [SMEM] + [VMEM] * 2
+    )(position, totals, start)
     return call(
         functools.partial(ratio_kernel, count),
         pltpu.HBM((total, cols), f32),
-        [SMEM] + [VMEM] * 11,
+        [VMEM] * 10,
         out_specs=HBM,
-        scratch=[pltpu.VMEM((total, cols), f32), pltpu.SemaphoreType.DMA((4,))],
-    )(position, totals, lta_start.reshape(1, cols), energy_before, head, rest, short_m, sums_m, rate,
+        scratch=[pltpu.VMEM((total, cols), f32), pltpu.SemaphoreType.DMA((12,))],
+    )(carry, energy_before, head, rest, short_m, sums_m, rate,
       scale, gain_scale, ends)
 
 

time: 63.9 us -> 62.9 us (0.984)
  blocking collectives: 29.3 us -> 45.9 us
  starting transfers between devices: 18 us -> 7.8 us
  waiting for transfers between devices: 8.03 us -> 0.01 us
    all_to_all x0 -> x1, blocking collectives: none -> 16.7 us  [body(): lax.all_to_all(totals, 'tm', split_axis=0, concat_axis=0, tiled=True)]
    all_to_all x1 -> x0, starting transfers between devices: 10.3 us -> none  [body(): lax.all_to_all(totals, 'tm', split_axis=0, concat_axis=0, tiled=True)]
    all_to_all x1 -> x0, waiting for transfers between devices: 8.02 us -> none  [body(): lax.all_to_all(totals, 'tm', split_axis=0, concat_axis=0, tiled=True)]
    pallas_call x1, Pallas kernels: 1.58 us -> 2.55 us  [body(): call(functools.partial(main_kernel, count), [struct((BLOCK, cols), bf16),...]
  transfers between devices with their start and end apart: 3 -> 2, of which waited for: 1 -> 0; matrix products, arithmetic and copies ran while one was open for 0% -> 0% of each run, Pallas kernels for 6% -> 7%
where the time goes in v3:
time: 62.9 us; the launch traced here: 62.6 us
  blocking collectives  45.9 us (73%)
  Pallas kernels  8.66 us (14%)
  starting transfers between devices  7.8 us (12%)
    all_to_all x1, blocking collectives, body(): lax.all_to_all(grouped, 'chan', split_axis=0, concat_axis=0, tiled=True)  29.2 us
    all_to_all x1, blocking collectives, body(): lax.all_to_all(totals, 'tm', split_axis=0, concat_axis=0, tiled=True)  16.7 us
    ppermute x2, starting transfers between devices, from_behind(): lax.ppermute(value, axis, [(source, source + 1) for source in range(count...  7.8 us
    pallas_call x1, Pallas kernels, body(): call(functools.partial(ratio_kernel, count), pltpu.HBM((total, cols), f32...  2.81 us
    pallas_call x1, Pallas kernels, body(): call(functools.partial(main_kernel, count), [struct((BLOCK, cols), bf16),...  2.55 us
    pallas_call x1, Pallas kernels, body(): call(regroup_kernel, pltpu.VMEM((parts, held, cols), bf16), [HBM], out_sp...  1.42 us
  transfers between devices with their start and end apart: 2, of which 0 were waited for; matrix products, arithmetic and copies ran while one was open for 0% of the time, Pallas kernels for 7%

profile of v3, /device:TPU:2, one launch (start us, length us, event | category | flops | bytes accessed | tf_op | source)
XLA Modules:
  0.0 62.6 jit_solution(5051034832038608459)
XLA Ops:
  0.0 1.4 %shard_map.82 = bf16[32,48,512]{2,1,0:T(8,128)(2,1)S(1)} custom-call(bf16[48,16384]{1,0:T(8,128)(2,1)} %raw.1), custom_call_target="tpu_custom_call" | custom-call | tf_op jit(solution)/shard_map/pallas_call | solution.py:246
  1.4 29.2 %all_to_all.10 = bf16[32,48,512]{2,1,0:T(8,128)(2,1)S(1)} all-to-all(bf16[32,48,512]{2,1,0:T(8,128)(2,1)S(1)} %shard_map.82), channel_id=1, replica_groups=mesh['tm'=8,'chan'=32] {'chan'}, dimensions={0} | all-to-all | bytes 3145728 | tf_op jit(solution)/shard_map/all_to_all | solution.py:253
  30.6 0.0 copy-start.5
  30.6 0.0 copy-start.6
  30.6 0.0 copy-start.8
  30.6 0.0 copy-start.9
  30.6 0.0 copy-start.10
  30.6 0.0 copy-start.11
  30.6 4.0 %collective-permute-start = (bf16[256,512]{1,0:T(8,128)(2,1)S(1)}, bf16[256,512]{1,0:T(8,128)(2,1)S(1)}, u32[]{:S(2)}, u32[]{:S(2)}) collective-permute-start(bf16[256,512]{1,0:T(8,128)(2,1)S(1)} %shard_map.83), channel_id=1, source_target_pairs={{0,32},{32,64},{64,96},{96,128},{128,160},{160,192},{192,224},{1,3... | collective-permute-start | bytes 786440 | tf_op jit(solution)/shard_map/ppermute | solution.py:37
  34.6 0.0 copy-done.5
  34.7 0.0 copy-done.6
  34.7 0.0 copy-done.8
  34.7 0.0 copy-done.9
  34.7 0.0 copy-done.10
  34.7 0.0 copy-done.11
  34.7 0.8 %shard_map.84 = (bf16[128,256]{1,0:T(8,128)(2,1)S(1)}, bf16[256,256]{1,0:T(8,128)(2,1)S(1)}, bf16[128,256]{1,0:T(8,128)(2,1)S(1)}, bf16[128,256]{1,0:T(8,128)(2,...) custom-call(bf16[1,128]{1,0:T(2,128)(2,1)S(1)} %bitcast.19, ...), custom_call_target="tpu_custom_call" | custom-call | tf_op jit(solution)/shard_map/pallas_call | solution.py:263
  35.6 0.0 copy-start.1
  35.6 0.0 copy-start.3
  35.6 2.5 %shard_map.85 = (bf16[128,512]{1,0:T(8,128)(2,1)S(1)}, bf16[1280,512]{1,0:T(8,128)(2,1)}, bf16[128,512]{1,0:T(8,128)(2,1)}, f32[20,512]{1,0:T(8,128)}) custom-call(bf16[1536,512]{1,0:T(8,128)(2,1)S(1)} %bitcast.11, bf16[128,256]{1,0:T(8,128)(2,1)S(1)} %get-tuple-element.35.band_m, bf16[256,256]{1,0:T(8,128)(2,1)S(1)} %get-tuple-element.36.pair_m, ...), custom_call_target="tpu_custom_call" | custom-call | tf_op jit(solution)/shard_map/pallas_call | solution.py:279
  38.1 0.0 copy-done.1
  38.1 0.0 copy-done.3
  38.1 3.8 %collective-permute-start.1 = (bf16[128,512]{1,0:T(8,128)(2,1)}, bf16[128,512]{1,0:T(8,128)(2,1)S(1)}, u32[]{:S(2)}, u32[]{:S(2)}) collective-permute-start(bf16[128,512]{1,0:T(8,128)(2,1)} %get-tuple-element.46), channel_id=1, source_target_pairs={{0,32},{32,64},{64,96},{96,128},{128,160},{160,192},{192,224},{1,3... | collective-permute-start | bytes 393224 | tf_op jit(solution)/shard_map/ppermute | solution.py:37
  42.0 0.0 collective-permute-done.prior_any
  42.0 0.0 copy-start.7
  42.0 0.0 copy-start
  42.0 0.0 copy-start.2
  42.0 0.0 copy-start.4
  42.0 1.0 %shard_map.86 = (bf16[256,512]{1,0:T(8,128)(2,1)S(1)}, f32[8,2,512]{2,1,0:T(2,128)S(1)}) custom-call(bf16[256,512]{1,0:T(8,128)(2,1)S(1)} %collective-permute-done.prior_any, bf16[1536,512]{1,0:T(8,128)(2,1)S(1)} %bitcast.12, bf16[128,512]{1,0:T(8,128)(2,1)S(1)} %get-tuple-element.39.band1, f32[20,512]{1,0:T(8,128)} %get-tuple-element.40.tails_hbm, ...), custom_call_target="tpu_custom_call" | custom-call | tf_op jit(solution)/shard_map/pallas_call | solution.py:297
  43.0 16.7 %all_to_all.11.totals = f32[8,2,512]{2,1,0:T(2,128)S(1)} all-to-all(f32[8,2,512]{2,1,0:T(2,128)S(1)} %get-tuple-element.44), channel_id=1, replica_groups=mesh['tm'=8,'chan'=32] {'tm'}, dimensions={0} | all-to-all | bytes 65536 | tf_op jit(solution)/shard_map/all_to_all | solution.py:311
  59.8 0.0 copy-done.7
  59.8 0.0 collective-permute-done.1.before
  59.8 0.0 copy-done
  59.8 0.0 copy-done.2
  59.8 0.0 copy-done.4
  59.8 2.8 %shard_map.88 = f32[1536,512]{1,0:T(8,128)} custom-call(f32[1,512]{1,0:T(1,128)S(1)} %shard_map.87.carry, bf16[128,512]{1,0:T(8,128)(2,1)S(1)} %collective-permute-done.1.before, bf16[256,512]{1,0:T(8,128)(2,1)S(1)} %get-tuple-element.47.head, bf16[1280,512]{1,0:T(8,128)(2,1)S(1)} %copy-done, bf16[128,256]{1,0:T(8,128)(2,1)S(1)} %copy-done.2, ...), custom_call_target="tpu_custom_call" | custom-call | tf_op jit(solution)/shard_map/pallas_call | solution.py:315
  (3 shorter events, 0.1 us)
Async XLA Ops:
  30.6 4.1 %copy-start.5 = (f32[512]{0:T(512)S(1)}, f32[512]{0:T(512)}, u32[]{:S(2)}) copy-start(f32[512]{0:T(512)} %param.13) | copy-start | bytes 6148
  30.6 4.1 %copy-start.6 = (f32[1536]{0:T(1024)S(1)}, f32[1536]{0:T(1024)}, u32[]{:S(2)}) copy-start(f32[1536]{0:T(1024)} %param.15) | copy-start | bytes 18436
  30.6 4.1 %copy-start.8 = (bf16[128]{0:T(256)(128)(2,1)S(1)}, bf16[128]{0:T(256)(128)(2,1)}, u32[]{:S(2)}) copy-start(bf16[128]{0:T(256)(128)(2,1)} %param.9) | copy-start | bytes 772
  30.6 4.1 %copy-start.9 = (bf16[128]{0:T(256)(128)(2,1)S(1)}, bf16[128]{0:T(256)(128)(2,1)}, u32[]{:S(2)}) copy-start(bf16[128]{0:T(256)(128)(2,1)} %param.10) | copy-start | bytes 772
  30.6 4.1 %copy-start.10 = (bf16[128]{0:T(256)(128)(2,1)S(1)}, bf16[128]{0:T(256)(128)(2,1)}, u32[]{:S(2)}) copy-start(bf16[128]{0:T(256)(128)(2,1)} %param.11) | copy-start | bytes 772
  30.6 4.1 %copy-start.11 = (bf16[128]{0:T(256)(128)(2,1)S(1)}, bf16[128]{0:T(256)(128)(2,1)}, u32[]{:S(2)}) copy-start(bf16[128]{0:T(256)(128)(2,1)} %param.12) | copy-start | bytes 772
  30.6 11.3 %collective-permute-start = (bf16[256,512]{1,0:T(8,128)(2,1)S(1)}, bf16[256,512]{1,0:T(8,128)(2,1)S(1)}, u32[]{:S(2)}, u32[]{:S(2)}) collective-permute-start(bf16[256,512]{1,0:T(8,128)(2,1)S(1)} %shard_map.83), channel_id=1, source_target_pairs={{0,32},{32,64},{64,96},{96,128},{128,160},{160,192},{192,224},{1,3... | collective-permute-start | bytes 786440 | tf_op jit(solution)/shard_map/ppermute | solution.py:37
  35.6 2.6 %copy-start.1 = (bf16[128,256]{1,0:T(8,128)(2,1)}, bf16[128,256]{1,0:T(8,128)(2,1)S(1)}, u32[]{:S(2)}) copy-start(bf16[128,256]{1,0:T(8,128)(2,1)S(1)} %get-tuple-element.49.short_m) | copy-start | bytes 196612
  35.6 2.6 %copy-start.3 = (bf16[128,256]{1,0:T(8,128)(2,1)}, bf16[128,256]{1,0:T(8,128)(2,1)S(1)}, u32[]{:S(2)}) copy-start(bf16[128,256]{1,0:T(8,128)(2,1)S(1)} %get-tuple-element.50.sums_m) | copy-start | bytes 196612
  38.1 21.6 %collective-permute-start.1 = (bf16[128,512]{1,0:T(8,128)(2,1)}, bf16[128,512]{1,0:T(8,128)(2,1)S(1)}, u32[]{:S(2)}, u32[]{:S(2)}) collective-permute-start(bf16[128,512]{1,0:T(8,128)(2,1)} %get-tuple-element.46), channel_id=1, source_target_pairs={{0,32},{32,64},{64,96},{96,128},{128,160},{160,192},{192,224},{1,3... | collective-permute-start | bytes 393224 | tf_op jit(solution)/shard_map/ppermute | solution.py:37
  42.0 17.8 %copy-start.7 = (f32[512]{0:T(512)S(1)}, f32[512]{0:T(512)}, u32[]{:S(2)}) copy-start(f32[512]{0:T(512)} %param.14) | copy-start | bytes 6148
  42.0 17.8 %copy-start = (bf16[1280,512]{1,0:T(8,128)(2,1)S(1)}, bf16[1280,512]{1,0:T(8,128)(2,1)}, u32[]{:S(2)}) copy-start(bf16[1280,512]{1,0:T(8,128)(2,1)} %get-tuple-element.48.rest) | copy-start | bytes 3932164
  42.0 17.8 %copy-start.2 = (bf16[128,256]{1,0:T(8,128)(2,1)S(1)}, bf16[128,256]{1,0:T(8,128)(2,1)}, u32[]{:S(2)}) copy-start(bf16[128,256]{1,0:T(8,128)(2,1)} %copy-done.1) | copy-start | bytes 196612
  42.0 17.8 %copy-start.4 = (bf16[128,256]{1,0:T(8,128)(2,1)S(1)}, bf16[128,256]{1,0:T(8,128)(2,1)}, u32[]{:S(2)}) copy-start(bf16[128,256]{1,0:T(8,128)(2,1)} %copy-done.3) | copy-start | bytes 196612

commit v4 on v3

--- a/solution.py
+++ b/solution.py
@@ -124,9 +124,19 @@
     return pl.ds(b * BLOCK, n * BLOCK)
 
 
+def compose(sums, ends):
+    value = jnp.zeros_like(ends[0:1, :])
+    decay = jnp.ones_like(value)
+    for s, row in sums:
+        step = ends[s : s + 1, :]
+        value = step * (value + row)
+        decay = decay * step
+    return jnp.concatenate([decay, value], axis=0)
+
+
 def main_kernel(
-    count, signal, band_m, pair_m, rate, scale, gain_scale, band1, energy, energy_last, tails, band,
-    energy_v, tails_v, sems,
+    count, signal, band_m, pair_m, rate, scale, gain_scale, ends, band1, energy, energy_last, tail, band,
+    energy_v, sems,
 ):
     for b in range(1, count):
         band[block(b), :] = dot(band_m[...], signal[block(b - 1, 2), :]).astype(jnp.bfloat16)
@@ -134,6 +144,7 @@
     order = [count - 1, *range(2, count - 1)]
     half = len(order) // 2
     copies = []
+    tails = {}
 
     def send(source, target):
         copy = pltpu.make_async_copy(source, target, sems.at[len(copies)])
@@ -145,27 +156,24 @@
         energy_v[block(b - 2), :] = e
         sums = last_sums(scaled_energy(e, rate[...], scale[...], gain_scale[block(b), :]))
         for h, row in enumerate(sums):
-            at = (b - 2) * len(sums) + h
-            tails_v[at : at + 1, :] = row
+            tails[b * len(sums) + h] = row
         if done == 0:
             send(energy_v.at[block(count - 3), :], energy_last)
         if done == half:
             send(energy_v.at[block(0, half), :], energy.at[block(0, half), :])
-    send(tails_v, tails)
     part = block(half, count - 2 - half)
     send(energy_v.at[part, :], energy.at[part, :])
+    tail[...] = compose(sorted(tails.items()), ends)
     for copy in copies:
         copy.wait()
 
 
 def edge_kernel(
-    subs, prior_any, signal, band1, tails_hbm, band_m, pair_m, rate, scale, gain_scale, ends,
-    energy, totals, window, tails, sems,
+    prior_any, signal, band1, tail, band_m, pair_m, rate, scale, gain_scale, ends,
+    energy, totals, window, sem,
 ):
-    copy = pltpu.make_async_copy(prior_any, window.at[block(0, 2), :], sems.at[0])
+    copy = pltpu.make_async_copy(prior_any, window.at[block(0, 2), :], sem)
     copy.start()
-    fetch = pltpu.make_async_copy(tails_hbm, tails, sems.at[1])
-    fetch.start()
     window[block(2), :] = signal[block(0), :]
     copy.wait()
     band = [
@@ -176,16 +184,9 @@
         e = energy_of(pair_m[...], jnp.concatenate([band[b], band[b + 1]], axis=0))
         energy[block(b), :] = e
         rows += last_sums(scaled_energy(e, rate[...], scale[...], gain_scale[block(b), :]))
-    edge = len(rows)
-    fetch.wait()
-    value = jnp.zeros_like(ends[0:1, :])
-    decay = jnp.ones_like(value)
-    for s in range(subs):
-        end = rows[s] if s < edge else tails[s - edge : s - edge + 1, :]
-        step = ends[s : s + 1, :]
-        value = step * (value + end)
-        decay = decay * step
-    both = jnp.concatenate([decay, value], axis=0)
+    first = compose(list(enumerate(rows)), ends)
+    decay, value = tail[0:1, :], tail[1:2, :]
+    both = jnp.concatenate([decay * first[0:1, :], decay * first[1:2, :] + value], axis=0)
     for k in range(totals.shape[0]):
         totals[k] = both
 
@@ -276,34 +277,29 @@
 
     halo = call(halo_kernel, pltpu.VMEM((2 * BLOCK, cols), bf16), [VMEM])(signal)
     prior = from_behind(halo, "tm")
-    band1, rest, energy_last, tails = call(
+    band1, rest, energy_last, tail = call(
         functools.partial(main_kernel, count),
         [
             struct((BLOCK, cols), bf16),
             pltpu.HBM((total - 2 * BLOCK, cols), bf16),
             pltpu.HBM((BLOCK, cols), bf16),
-            pltpu.HBM((subs - 2 * BLOCK // SUB, cols), f32),
+            struct((2, cols), f32),
         ],
-        [VMEM] * 6,
-        out_specs=[VMEM, HBM, HBM, HBM],
+        [VMEM] * 7,
+        out_specs=[VMEM, HBM, HBM, VMEM],
         scratch=[
             pltpu.VMEM((total, cols), bf16),
             pltpu.VMEM((total - 2 * BLOCK, cols), bf16),
-            pltpu.VMEM((subs - 2 * BLOCK // SUB, cols), f32),
-            pltpu.SemaphoreType.DMA((4,)),
+            pltpu.SemaphoreType.DMA((3,)),
         ],
-    )(signal, band_m, pair_m, rate, scale, gain_scale)
+    )(signal, band_m, pair_m, rate, scale, gain_scale, ends)
     energy_before = from_behind(energy_last, "tm")
     head, totals = call(
-        functools.partial(edge_kernel, subs),
+        edge_kernel,
         [struct((2 * BLOCK, cols), bf16), pltpu.VMEM((groups, 2, cols), f32)],
-        [ANY] + [VMEM] * 2 + [HBM] + [VMEM] * 6,
-        scratch=[
-            pltpu.VMEM((3 * BLOCK, cols), bf16),
-            pltpu.VMEM((subs - 2 * BLOCK // SUB, cols), f32),
-            pltpu.SemaphoreType.DMA((2,)),
-        ],
-    )(prior, signal, band1, hbm(tails), band_m, pair_m, rate, scale, gain_scale, ends)
+        [ANY] + [VMEM] * 9,
+        scratch=[pltpu.VMEM((3 * BLOCK, cols), bf16), pltpu.SemaphoreType.DMA],
+    )(prior, signal, band1, tail, band_m, pair_m, rate, scale, gain_scale, ends)
     position = lax.axis_index("tm").astype(jnp.int32).reshape(1)
     totals, position, start = lax.optimization_barrier(
         (totals, position, lta_start.reshape(1, cols))

time: 62.9 us -> 62.5 us (level)
  no operation moved by 1% of the time
where the time goes in v4:
time: 62.5 us; the launch traced here: 62.2 us
  blocking collectives  45.8 us (73%)
  Pallas kernels  8.27 us (13%)
  starting transfers between devices  7.8 us (12%)
    all_to_all x1, blocking collectives, body(): lax.all_to_all(grouped, 'chan', split_axis=0, concat_axis=0, tiled=True)  29.2 us
    all_to_all x1, blocking collectives, body(): lax.all_to_all(totals, 'tm', split_axis=0, concat_axis=0, tiled=True)  16.7 us
    ppermute x2, starting transfers between devices, from_behind(): lax.ppermute(value, axis, [(source, source + 1) for source in range(count...  7.8 us
    pallas_call x1, Pallas kernels, body(): call(functools.partial(ratio_kernel, count), pltpu.HBM((total, cols), f32...  2.79 us
    pallas_call x1, Pallas kernels, body(): call(functools.partial(main_kernel, count), [struct((BLOCK, cols), bf16),...  2.56 us
    pallas_call x1, Pallas kernels, body(): call(regroup_kernel, pltpu.VMEM((parts, held, cols), bf16), [HBM], out_sp...  1.42 us
  transfers between devices with their start and end apart: 2, of which 0 were waited for; matrix products, arithmetic and copies ran while one was open for 0% of the time, Pallas kernels for 7%

profile of v4, /device:TPU:2, one launch (start us, length us, event | category | flops | bytes accessed | tf_op | source)
XLA Modules:
  0.0 62.2 jit_solution(14305100350908751404)
XLA Ops:
  0.0 1.4 %shard_map.82 = bf16[32,48,512]{2,1,0:T(8,128)(2,1)S(1)} custom-call(bf16[48,16384]{1,0:T(8,128)(2,1)} %raw.1), custom_call_target="tpu_custom_call" | custom-call | tf_op jit(solution)/shard_map/pallas_call | solution.py:247
  1.4 29.2 %all_to_all.10 = bf16[32,48,512]{2,1,0:T(8,128)(2,1)S(1)} all-to-all(bf16[32,48,512]{2,1,0:T(8,128)(2,1)S(1)} %shard_map.82), channel_id=1, replica_groups=mesh['tm'=8,'chan'=32] {'chan'}, dimensions={0} | all-to-all | bytes 3145728 | tf_op jit(solution)/shard_map/all_to_all | solution.py:254
  30.6 0.0 copy-start.5
  30.6 0.0 copy-start.6
  30.6 0.0 copy-start.8
  30.6 0.0 copy-start.9
  30.6 0.0 copy-start.10
  30.6 0.0 copy-start.11
  30.6 4.0 %collective-permute-start = (bf16[256,512]{1,0:T(8,128)(2,1)S(1)}, bf16[256,512]{1,0:T(8,128)(2,1)S(1)}, u32[]{:S(2)}, u32[]{:S(2)}) collective-permute-start(bf16[256,512]{1,0:T(8,128)(2,1)S(1)} %shard_map.83), channel_id=1, source_target_pairs={{0,32},{32,64},{64,96},{96,128},{128,160},{160,192},{192,224},{1,3... | collective-permute-start | bytes 786440 | tf_op jit(solution)/shard_map/ppermute | solution.py:37
  34.6 0.0 copy-done.5
  34.7 0.0 copy-done.6
  34.7 0.0 copy-done.8
  34.7 0.0 copy-done.9
  34.7 0.0 copy-done.10
  34.7 0.0 copy-done.11
  34.7 0.8 %shard_map.84 = (bf16[128,256]{1,0:T(8,128)(2,1)S(1)}, bf16[256,256]{1,0:T(8,128)(2,1)S(1)}, bf16[128,256]{1,0:T(8,128)(2,1)S(1)}, bf16[128,256]{1,0:T(8,128)(2,...) custom-call(bf16[1,128]{1,0:T(2,128)(2,1)S(1)} %bitcast.19, ...), custom_call_target="tpu_custom_call" | custom-call | tf_op jit(solution)/shard_map/pallas_call | solution.py:264
  35.6 0.0 copy-start.1
  35.6 0.0 copy-start.3
  35.6 2.6 %shard_map.85 = (bf16[128,512]{1,0:T(8,128)(2,1)S(1)}, bf16[1280,512]{1,0:T(8,128)(2,1)}, bf16[128,512]{1,0:T(8,128)(2,1)}, f32[2,512]{1,0:T(2,128)S(1)}) custom-call(bf16[1536,512]{1,0:T(8,128)(2,1)S(1)} %bitcast.11, bf16[128,256]{1,0:T(8,128)(2,1)S(1)} %get-tuple-element.35.band_m, bf16[256,256]{1,0:T(8,128)(2,1)S(1)} %get-tuple-element.36.pair_m, ...), custom_call_target="tpu_custom_call" | custom-call | tf_op jit(solution)/shard_map/pallas_call | solution.py:280
  38.1 0.0 copy-done.1
  38.2 0.0 copy-done.3
  38.2 3.8 %collective-permute-start.1 = (bf16[128,512]{1,0:T(8,128)(2,1)}, bf16[128,512]{1,0:T(8,128)(2,1)S(1)}, u32[]{:S(2)}, u32[]{:S(2)}) collective-permute-start(bf16[128,512]{1,0:T(8,128)(2,1)} %get-tuple-element.46), channel_id=1, source_target_pairs={{0,32},{32,64},{64,96},{96,128},{128,160},{160,192},{192,224},{1,3... | collective-permute-start | bytes 393224 | tf_op jit(solution)/shard_map/ppermute | solution.py:37
  42.0 0.0 collective-permute-done.prior_any
  42.0 0.0 copy-start.7
  42.0 0.0 copy-start
  42.0 0.0 copy-start.2
  42.0 0.0 copy-start.4
  42.0 0.6 %shard_map.86 = (bf16[256,512]{1,0:T(8,128)(2,1)S(1)}, f32[8,2,512]{2,1,0:T(2,128)S(1)}) custom-call(bf16[256,512]{1,0:T(8,128)(2,1)S(1)} %collective-permute-done.prior_any, bf16[1536,512]{1,0:T(8,128)(2,1)S(1)} %bitcast.12, bf16[128,512]{1,0:T(8,128)(2,1)S(1)} %get-tuple-element.40.band1, f32[2,512]{1,0:T(2,128)S(1)} %get-tuple-element.41.tail, ...), custom_call_target="tpu_custom_call" | custom-call | tf_op jit(solution)/shard_map/pallas_call | solution.py:297
  42.7 16.7 %all_to_all.11.totals = f32[8,2,512]{2,1,0:T(2,128)S(1)} all-to-all(f32[8,2,512]{2,1,0:T(2,128)S(1)} %get-tuple-element.44), channel_id=1, replica_groups=mesh['tm'=8,'chan'=32] {'tm'}, dimensions={0} | all-to-all | bytes 65536 | tf_op jit(solution)/shard_map/all_to_all | solution.py:307
  59.4 0.0 copy-done.7
  59.4 0.0 collective-permute-done.1.before
  59.4 0.0 copy-done
  59.4 0.0 copy-done.2
  59.4 0.0 copy-done.4
  59.4 2.8 %shard_map.88 = f32[1536,512]{1,0:T(8,128)} custom-call(f32[1,512]{1,0:T(1,128)S(1)} %shard_map.87.carry, bf16[128,512]{1,0:T(8,128)(2,1)S(1)} %collective-permute-done.1.before, bf16[256,512]{1,0:T(8,128)(2,1)S(1)} %get-tuple-element.47.head, bf16[1280,512]{1,0:T(8,128)(2,1)S(1)} %copy-done, bf16[128,256]{1,0:T(8,128)(2,1)S(1)} %copy-done.2, ...), custom_call_target="tpu_custom_call" | custom-call | tf_op jit(solution)/shard_map/pallas_call | solution.py:311
  (3 shorter events, 0.1 us)
Async XLA Ops:
  30.6 4.1 %copy-start.5 = (f32[512]{0:T(512)S(1)}, f32[512]{0:T(512)}, u32[]{:S(2)}) copy-start(f32[512]{0:T(512)} %param.13) | copy-start | bytes 6148
  30.6 4.1 %copy-start.6 = (f32[1536]{0:T(1024)S(1)}, f32[1536]{0:T(1024)}, u32[]{:S(2)}) copy-start(f32[1536]{0:T(1024)} %param.15) | copy-start | bytes 18436
  30.6 4.1 %copy-start.8 = (bf16[128]{0:T(256)(128)(2,1)S(1)}, bf16[128]{0:T(256)(128)(2,1)}, u32[]{:S(2)}) copy-start(bf16[128]{0:T(256)(128)(2,1)} %param.9) | copy-start | bytes 772
  30.6 4.1 %copy-start.9 = (bf16[128]{0:T(256)(128)(2,1)S(1)}, bf16[128]{0:T(256)(128)(2,1)}, u32[]{:S(2)}) copy-start(bf16[128]{0:T(256)(128)(2,1)} %param.10) | copy-start | bytes 772
  30.6 4.1 %copy-start.10 = (bf16[128]{0:T(256)(128)(2,1)S(1)}, bf16[128]{0:T(256)(128)(2,1)}, u32[]{:S(2)}) copy-start(bf16[128]{0:T(256)(128)(2,1)} %param.11) | copy-start | bytes 772
  30.6 4.1 %copy-start.11 = (bf16[128]{0:T(256)(128)(2,1)S(1)}, bf16[128]{0:T(256)(128)(2,1)}, u32[]{:S(2)}) copy-start(bf16[128]{0:T(256)(128)(2,1)} %param.12) | copy-start | bytes 772
  30.6 11.4 %collective-permute-start = (bf16[256,512]{1,0:T(8,128)(2,1)S(1)}, bf16[256,512]{1,0:T(8,128)(2,1)S(1)}, u32[]{:S(2)}, u32[]{:S(2)}) collective-permute-start(bf16[256,512]{1,0:T(8,128)(2,1)S(1)} %shard_map.83), channel_id=1, source_target_pairs={{0,32},{32,64},{64,96},{96,128},{128,160},{160,192},{192,224},{1,3... | collective-permute-start | bytes 786440 | tf_op jit(solution)/shard_map/ppermute | solution.py:37
  35.6 2.6 %copy-start.1 = (bf16[128,256]{1,0:T(8,128)(2,1)}, bf16[128,256]{1,0:T(8,128)(2,1)S(1)}, u32[]{:S(2)}) copy-start(bf16[128,256]{1,0:T(8,128)(2,1)S(1)} %get-tuple-element.49.short_m) | copy-start | bytes 196612
  35.6 2.6 %copy-start.3 = (bf16[128,256]{1,0:T(8,128)(2,1)}, bf16[128,256]{1,0:T(8,128)(2,1)S(1)}, u32[]{:S(2)}) copy-start(bf16[128,256]{1,0:T(8,128)(2,1)S(1)} %get-tuple-element.50.sums_m) | copy-start | bytes 196612
  38.2 21.2 %collective-permute-start.1 = (bf16[128,512]{1,0:T(8,128)(2,1)}, bf16[128,512]{1,0:T(8,128)(2,1)S(1)}, u32[]{:S(2)}, u32[]{:S(2)}) collective-permute-start(bf16[128,512]{1,0:T(8,128)(2,1)} %get-tuple-element.46), channel_id=1, source_target_pairs={{0,32},{32,64},{64,96},{96,128},{128,160},{160,192},{192,224},{1,3... | collective-permute-start | bytes 393224 | tf_op jit(solution)/shard_map/ppermute | solution.py:37
  42.0 17.4 %copy-start.7 = (f32[512]{0:T(512)S(1)}, f32[512]{0:T(512)}, u32[]{:S(2)}) copy-start(f32[512]{0:T(512)} %param.14) | copy-start | bytes 6148
  42.0 17.4 %copy-start = (bf16[1280,512]{1,0:T(8,128)(2,1)S(1)}, bf16[1280,512]{1,0:T(8,128)(2,1)}, u32[]{:S(2)}) copy-start(bf16[1280,512]{1,0:T(8,128)(2,1)} %get-tuple-element.48.rest) | copy-start | bytes 3932164
  42.0 17.4 %copy-start.2 = (bf16[128,256]{1,0:T(8,128)(2,1)S(1)}, bf16[128,256]{1,0:T(8,128)(2,1)}, u32[]{:S(2)}) copy-start(bf16[128,256]{1,0:T(8,128)(2,1)} %copy-done.1) | copy-start | bytes 196612
  42.0 17.4 %copy-start.4 = (bf16[128,256]{1,0:T(8,128)(2,1)S(1)}, bf16[128,256]{1,0:T(8,128)(2,1)}, u32[]{:S(2)}) copy-start(bf16[128,256]{1,0:T(8,128)(2,1)} %copy-done.3) | copy-start | bytes 196612

commit v5 on v4

--- a/solution.py
+++ b/solution.py
@@ -169,16 +169,11 @@
 
 
 def edge_kernel(
-    prior_any, signal, band1, tail, band_m, pair_m, rate, scale, gain_scale, ends,
-    energy, totals, window, sem,
+    prior, signal, band1, tail, band_m, pair_m, rate, scale, gain_scale, ends,
+    energy, totals,
 ):
-    copy = pltpu.make_async_copy(prior_any, window.at[block(0, 2), :], sem)
-    copy.start()
-    window[block(2), :] = signal[block(0), :]
-    copy.wait()
-    band = [
-        dot(band_m[...], window[block(b, 2), :]).astype(jnp.bfloat16) for b in range(2)
-    ] + [band1[...]]
+    windows = [prior[...], jnp.concatenate([prior[block(1), :], signal[block(0), :]], axis=0)]
+    band = [dot(band_m[...], window).astype(jnp.bfloat16) for window in windows] + [band1[...]]
     rows = []
     for b in range(2):
         e = energy_of(pair_m[...], jnp.concatenate([band[b], band[b + 1]], axis=0))
@@ -297,8 +292,7 @@
     head, totals = call(
         edge_kernel,
         [struct((2 * BLOCK, cols), bf16), pltpu.VMEM((groups, 2, cols), f32)],
-        [ANY] + [VMEM] * 9,
-        scratch=[pltpu.VMEM((3 * BLOCK, cols), bf16), pltpu.SemaphoreType.DMA],
+        [VMEM] * 10,
     )(prior, signal, band1, tail, band_m, pair_m, rate, scale, gain_scale, ends)
     position = lax.axis_index("tm").astype(jnp.int32).reshape(1)
     totals, position, start = lax.optimization_barrier(

time: 62.5 us -> 62.4 us (level)
  transfers between devices with their start and end apart: 2 -> 2, of which waited for: 0 -> 0; matrix products, arithmetic and copies ran while one was open for 0% -> 0% of each run, Pallas kernels for 7% -> 6%
where the time goes in v5:
time: 62.4 us; the launch traced here: 62.2 us
  blocking collectives  45.9 us (74%)
  Pallas kernels  8.23 us (13%)
  starting transfers between devices  7.8 us (12%)
    all_to_all x1, blocking collectives, body(): lax.all_to_all(grouped, 'chan', split_axis=0, concat_axis=0, tiled=True)  29.2 us
    all_to_all x1, blocking collectives, body(): lax.all_to_all(totals, 'tm', split_axis=0, concat_axis=0, tiled=True)  16.7 us
    ppermute x2, starting transfers between devices, from_behind(): lax.ppermute(value, axis, [(source, source + 1) for source in range(count...  7.8 us
    pallas_call x1, Pallas kernels, body(): call(functools.partial(ratio_kernel, count), pltpu.HBM((total, cols), f32...  2.79 us
    pallas_call x1, Pallas kernels, body(): call(functools.partial(main_kernel, count), [struct((BLOCK, cols), bf16),...  2.56 us
    pallas_call x1, Pallas kernels, body(): call(regroup_kernel, pltpu.VMEM((parts, held, cols), bf16), [HBM], out_sp...  1.42 us
  transfers between devices with their start and end apart: 2, of which 0 were waited for; matrix products, arithmetic and copies ran while one was open for 0% of the time, Pallas kernels for 6%

profile of v5, /device:TPU:2, one launch (start us, length us, event | category | flops | bytes accessed | tf_op | source)
XLA Modules:
  0.0 62.2 jit_solution(2879334870395053073)
XLA Ops:
  0.0 1.4 %shard_map.82 = bf16[32,48,512]{2,1,0:T(8,128)(2,1)S(1)} custom-call(bf16[48,16384]{1,0:T(8,128)(2,1)} %raw.1), custom_call_target="tpu_custom_call" | custom-call | tf_op jit(solution)/shard_map/pallas_call | solution.py:242
  1.4 29.2 %all_to_all.10 = bf16[32,48,512]{2,1,0:T(8,128)(2,1)S(1)} all-to-all(bf16[32,48,512]{2,1,0:T(8,128)(2,1)S(1)} %shard_map.82), channel_id=1, replica_groups=mesh['tm'=8,'chan'=32] {'chan'}, dimensions={0} | all-to-all | bytes 3145728 | tf_op jit(solution)/shard_map/all_to_all | solution.py:249
  30.6 0.0 copy-start.5
  30.6 0.0 copy-start.6
  30.6 0.0 copy-start.8
  30.6 0.0 copy-start.9
  30.6 0.0 copy-start.10
  30.6 0.0 copy-start.11
  30.6 4.0 %collective-permute-start = (bf16[256,512]{1,0:T(8,128)(2,1)S(1)}, bf16[256,512]{1,0:T(8,128)(2,1)S(1)}, u32[]{:S(2)}, u32[]{:S(2)}) collective-permute-start(bf16[256,512]{1,0:T(8,128)(2,1)S(1)} %shard_map.83), channel_id=1, source_target_pairs={{0,32},{32,64},{64,96},{96,128},{128,160},{160,192},{192,224},{1,3... | collective-permute-start | bytes 786440 | tf_op jit(solution)/shard_map/ppermute | solution.py:37
  34.6 0.0 copy-done.5
  34.7 0.0 copy-done.6
  34.7 0.0 copy-done.8
  34.7 0.0 copy-done.9
  34.7 0.0 copy-done.10
  34.7 0.0 copy-done.11
  34.7 0.8 %shard_map.84 = (bf16[128,256]{1,0:T(8,128)(2,1)S(1)}, bf16[256,256]{1,0:T(8,128)(2,1)S(1)}, bf16[128,256]{1,0:T(8,128)(2,1)S(1)}, bf16[128,256]{1,0:T(8,128)(2,...) custom-call(bf16[1,128]{1,0:T(2,128)(2,1)S(1)} %bitcast.19, ...), custom_call_target="tpu_custom_call" | custom-call | tf_op jit(solution)/shard_map/pallas_call | solution.py:259
  35.6 0.0 copy-start.1
  35.6 0.0 copy-start.3
  35.6 2.6 %shard_map.85 = (bf16[128,512]{1,0:T(8,128)(2,1)S(1)}, bf16[1280,512]{1,0:T(8,128)(2,1)}, bf16[128,512]{1,0:T(8,128)(2,1)}, f32[2,512]{1,0:T(2,128)S(1)}) custom-call(bf16[1536,512]{1,0:T(8,128)(2,1)S(1)} %bitcast.11, bf16[128,256]{1,0:T(8,128)(2,1)S(1)} %get-tuple-element.35.band_m, bf16[256,256]{1,0:T(8,128)(2,1)S(1)} %get-tuple-element.36.pair_m, ...), custom_call_target="tpu_custom_call" | custom-call | tf_op jit(solution)/shard_map/pallas_call | solution.py:275
  38.1 0.0 copy-done.1
  38.2 0.0 copy-done.3
  38.2 3.8 %collective-permute-start.1 = (bf16[128,512]{1,0:T(8,128)(2,1)}, bf16[128,512]{1,0:T(8,128)(2,1)S(1)}, u32[]{:S(2)}, u32[]{:S(2)}) collective-permute-start(bf16[128,512]{1,0:T(8,128)(2,1)} %get-tuple-element.46), channel_id=1, source_target_pairs={{0,32},{32,64},{64,96},{96,128},{128,160},{160,192},{192,224},{1,3... | collective-permute-start | bytes 393224 | tf_op jit(solution)/shard_map/ppermute | solution.py:37
  42.0 0.0 collective-permute-done.prior
  42.0 0.0 copy-start.7
  42.0 0.0 copy-start
  42.0 0.0 copy-start.2
  42.0 0.0 copy-start.4
  42.0 0.6 shard_map.86
  42.6 16.7 %all_to_all.11.totals = f32[8,2,512]{2,1,0:T(2,128)S(1)} all-to-all(f32[8,2,512]{2,1,0:T(2,128)S(1)} %get-tuple-element.44), channel_id=1, replica_groups=mesh['tm'=8,'chan'=32] {'tm'}, dimensions={0} | all-to-all | bytes 65536 | tf_op jit(solution)/shard_map/all_to_all | solution.py:301
  59.3 0.0 copy-done.7
  59.4 0.0 collective-permute-done.1.before
  59.4 0.0 copy-done
  59.4 0.0 copy-done.2
  59.4 0.0 copy-done.4
  59.4 2.8 %shard_map.88 = f32[1536,512]{1,0:T(8,128)} custom-call(f32[1,512]{1,0:T(1,128)S(1)} %shard_map.87.carry, bf16[128,512]{1,0:T(8,128)(2,1)S(1)} %collective-permute-done.1.before, bf16[256,512]{1,0:T(8,128)(2,1)S(1)} %get-tuple-element.47.head, bf16[1280,512]{1,0:T(8,128)(2,1)S(1)} %copy-done, bf16[128,256]{1,0:T(8,128)(2,1)S(1)} %copy-done.2, ...), custom_call_target="tpu_custom_call" | custom-call | tf_op jit(solution)/shard_map/pallas_call | solution.py:305
  (3 shorter events, 0.1 us)
Async XLA Ops:
  30.6 4.1 %copy-start.5 = (f32[512]{0:T(512)S(1)}, f32[512]{0:T(512)}, u32[]{:S(2)}) copy-start(f32[512]{0:T(512)} %param.13) | copy-start | bytes 6148
  30.6 4.1 %copy-start.6 = (f32[1536]{0:T(1024)S(1)}, f32[1536]{0:T(1024)}, u32[]{:S(2)}) copy-start(f32[1536]{0:T(1024)} %param.15) | copy-start | bytes 18436
  30.6 4.1 %copy-start.8 = (bf16[128]{0:T(256)(128)(2,1)S(1)}, bf16[128]{0:T(256)(128)(2,1)}, u32[]{:S(2)}) copy-start(bf16[128]{0:T(256)(128)(2,1)} %param.9) | copy-start | bytes 772
  30.6 4.1 %copy-start.9 = (bf16[128]{0:T(256)(128)(2,1)S(1)}, bf16[128]{0:T(256)(128)(2,1)}, u32[]{:S(2)}) copy-start(bf16[128]{0:T(256)(128)(2,1)} %param.10) | copy-start | bytes 772
  30.6 4.1 %copy-start.10 = (bf16[128]{0:T(256)(128)(2,1)S(1)}, bf16[128]{0:T(256)(128)(2,1)}, u32[]{:S(2)}) copy-start(bf16[128]{0:T(256)(128)(2,1)} %param.11) | copy-start | bytes 772
  30.6 4.1 %copy-start.11 = (bf16[128]{0:T(256)(128)(2,1)S(1)}, bf16[128]{0:T(256)(128)(2,1)}, u32[]{:S(2)}) copy-start(bf16[128]{0:T(256)(128)(2,1)} %param.12) | copy-start | bytes 772
  30.6 11.4 %collective-permute-start = (bf16[256,512]{1,0:T(8,128)(2,1)S(1)}, bf16[256,512]{1,0:T(8,128)(2,1)S(1)}, u32[]{:S(2)}, u32[]{:S(2)}) collective-permute-start(bf16[256,512]{1,0:T(8,128)(2,1)S(1)} %shard_map.83), channel_id=1, source_target_pairs={{0,32},{32,64},{64,96},{96,128},{128,160},{160,192},{192,224},{1,3... | collective-permute-start | bytes 786440 | tf_op jit(solution)/shard_map/ppermute | solution.py:37
  35.6 2.6 %copy-start.1 = (bf16[128,256]{1,0:T(8,128)(2,1)}, bf16[128,256]{1,0:T(8,128)(2,1)S(1)}, u32[]{:S(2)}) copy-start(bf16[128,256]{1,0:T(8,128)(2,1)S(1)} %get-tuple-element.49.short_m) | copy-start | bytes 196612
  35.6 2.6 %copy-start.3 = (bf16[128,256]{1,0:T(8,128)(2,1)}, bf16[128,256]{1,0:T(8,128)(2,1)S(1)}, u32[]{:S(2)}) copy-start(bf16[128,256]{1,0:T(8,128)(2,1)S(1)} %get-tuple-element.50.sums_m) | copy-start | bytes 196612
  38.2 21.2 %collective-permute-start.1 = (bf16[128,512]{1,0:T(8,128)(2,1)}, bf16[128,512]{1,0:T(8,128)(2,1)S(1)}, u32[]{:S(2)}, u32[]{:S(2)}) collective-permute-start(bf16[128,512]{1,0:T(8,128)(2,1)} %get-tuple-element.46), channel_id=1, source_target_pairs={{0,32},{32,64},{64,96},{96,128},{128,160},{160,192},{192,224},{1,3... | collective-permute-start | bytes 393224 | tf_op jit(solution)/shard_map/ppermute | solution.py:37
  42.0 17.3 %copy-start.7 = (f32[512]{0:T(512)S(1)}, f32[512]{0:T(512)}, u32[]{:S(2)}) copy-start(f32[512]{0:T(512)} %param.14) | copy-start | bytes 6148
  42.0 17.4 %copy-start = (bf16[1280,512]{1,0:T(8,128)(2,1)S(1)}, bf16[1280,512]{1,0:T(8,128)(2,1)}, u32[]{:S(2)}) copy-start(bf16[1280,512]{1,0:T(8,128)(2,1)} %get-tuple-element.48.rest) | copy-start | bytes 3932164
  42.0 17.4 %copy-start.2 = (bf16[128,256]{1,0:T(8,128)(2,1)S(1)}, bf16[128,256]{1,0:T(8,128)(2,1)}, u32[]{:S(2)}) copy-start(bf16[128,256]{1,0:T(8,128)(2,1)} %copy-done.1) | copy-start | bytes 196612
  42.0 17.4 %copy-start.4 = (bf16[128,256]{1,0:T(8,128)(2,1)S(1)}, bf16[128,256]{1,0:T(8,128)(2,1)}, u32[]{:S(2)}) copy-start(bf16[128,256]{1,0:T(8,128)(2,1)} %copy-done.3) | copy-start | bytes 196612
